TPU v7x, 512 devices: a whole 4x4x16 slice. The times are simulated.
512 devices in a mesh: replica: 32 (over x, z_lo), fsdp: 16 (over z_hi, y, core).
Axes of the slice: x: 4, y: 4, z: 16 (z_hi: 2, z_lo: 8; z = z_hi * 8 + z_lo), core: 2. Of those that a mesh axis runs over, the one named last changes fastest.
Arguments:
- acts: bfloat16 [65536, 8192], P(('replica', 'fsdp')), may hold values from -6 to 6
- norm_gain: bfloat16 [8192], replicated, may hold values from 0.099609375 to 1.8984375
- key_weight: bfloat16 [32, 8192, 512], P('replica', 'fsdp'), may hold values from -6 to 6
- key_cotangent: bfloat16 [65536, 512], P(('replica', 'fsdp')), may hold values from -6 to 6
- pending_delta: bfloat16 [32, 8192, 128], P('replica', 'fsdp'), may hold values from -6 to 6
- fragment_index: int32 [1], replicated, may hold values from 0 to 384
- global_frag: float32 [8192, 128], P('fsdp'), may hold values from -6 to 6
- outer_mom: float32 [8192, 128], P('fsdp'), may hold values from -3 to 3
Outputs:
- key_out: bfloat16 [65536, 512], P(('replica', 'fsdp'))
- new_weight: bfloat16 [32, 8192, 512], P('replica', 'fsdp')
- global_new: float32 [8192, 128], P('fsdp')
- mom_new: float32 [8192, 128], P('fsdp')
All inputs are finite; a program needn't handle non-finite values.
Results may differ from a plain program's by a relative error of at most 0.015.
Values may be sent and summed in bfloat16 or wider, within the bound.
No kernel may reach another device: no remote copies, remote signals or barrier semaphores. Data moves between devices by JAX's collectives and lax.ppermute only.
A program may use at most 64 MiB of HBM per device.

v0:
```python
import jax
import jax.numpy as jnp
from jax import lax
from jax.sharding import PartitionSpec as P

D = 8192


inner_rate = 0.5
outer_rate = 0.7
momentum_coef = 0.9
blend_coef = 0.5


def place_fragment(global_new, start, kv_width):
    placed = jnp.zeros((global_new.shape[0], kv_width), global_new.dtype)
    placed = lax.dynamic_update_slice(placed, global_new, (jnp.zeros((), jnp.int32), start))
    column = lax.broadcasted_iota(jnp.int32, (1, kv_width), 1) - start
    inside = (column >= 0) & (column < global_new.shape[1])
    return (placed, inside)


def body(
    acts,
    norm_gain,
    key_weight,
    key_cotangent,
    pending_delta,
    fragment_index,
    global_frag,
    outer_mom,
):
    token_rows = acts.astype(jnp.float32)
    rms_scale = lax.rsqrt(jnp.mean(token_rows * token_rows, axis=-1, keepdims=True) + 1e-05)
    normed = (token_rows * rms_scale * norm_gain.astype(jnp.float32)).astype(jnp.bfloat16)
    inverse_root = D ** (-0.5)
    kv_width = key_weight.shape[2]
    columns = lax.all_to_all(normed, "fsdp", split_axis=1, concat_axis=0, tiled=True)
    slab = normed
    summed_keys = jnp.dot(
        slab,
        lax.all_gather(key_weight, "fsdp", axis=1, tiled=True)[0],
        preferred_element_type=jnp.float32,
    )
    key_out = (summed_keys * inverse_root).astype(jnp.bfloat16)
    slab = columns
    gradient = (
        lax.dot_general(
            slab,
            lax.all_gather(key_cotangent, "fsdp", axis=0, tiled=True),
            (((0,), (0,)), ((), ())),
            preferred_element_type=jnp.float32,
        )
        * inverse_root
    )
    stepped = key_weight[0].astype(jnp.float32) - inner_rate * gradient
    replicas = lax.axis_size("replica")
    summed_delta = lax.psum(
        pending_delta[0].astype(jnp.float32).astype(jnp.bfloat16), "replica"
    ).astype(jnp.float32)
    mean_delta = summed_delta / replicas
    mom_new = momentum_coef * outer_mom + mean_delta
    global_new = global_frag - outer_rate * (momentum_coef * mom_new + mean_delta)
    placed, in_fragment = place_fragment(global_new, fragment_index[0], kv_width)
    blended = jnp.where(in_fragment, blend_coef * stepped + (1.0 - blend_coef) * placed, stepped)
    new_weight = blended.astype(jnp.bfloat16)[None]
    return (key_out, new_weight, global_new, mom_new)


def solution(mesh):
    in_specs = (
        P(("replica", "fsdp"), None),
        P(),
        P("replica", "fsdp", None),
        P(("replica", "fsdp"), None),
        P("replica", "fsdp", None),
        P(),
        P("fsdp", None),
        P("fsdp", None),
    )
    out_specs = (
        P(("replica", "fsdp"), None),
        P("replica", "fsdp", None),
        P("fsdp", None),
        P("fsdp", None),
    )
    return jax.shard_map(body, mesh=mesh, in_specs=in_specs, out_specs=out_specs, check_vma=False)
```

profile of v0, /device:TPU:8, one launch (start us, length us, event | category | flops | bytes accessed | tf_op | source)
XLA Modules:
  0.0 640.7 jit_solution(2104903293980288000)
XLA Ops:
  8.0 0.0 all-gather.5.cloned.1.call-start
  8.0 0.7 all-gather.5.cloned.1.call-update
  8.7 0.0 all-reduce.2.cloned.1.call-start
  8.8 0.5 all-reduce.2.cloned.1.call-update
  9.3 0.0 all-gather.3.cloned.1.call-start
  9.4 0.7 all-gather.3.cloned.1.call-update
  10.1 0.0 copy-start.3
  10.1 3.2 copy.12
  13.3 0.0 copy-done.3
  13.3 1.1 fusion.2
  14.4 4.3 fusion.4
  18.8 18.2 %all-to-all-start = ((bf16[128,16,512]{0,2,1:T(8,128)(2,1)}), bf16[128,16,512]{0,2,1:T(8,128)(2,1)S(1)}, u32[]{:S(2)}, u32[]{:S(2)}) async-start(bf16[128,16,512]{0,2,1:T(8,128)(2,1)} %bitcast.3), calls=%async_computation | async-start | bytes 4194304 | tf_op jit(solution)/shard_map/all_to_all | solution.py:38
  37.6 75.8 %all-to-all-done = bf16[128,16,512]{0,2,1:T(8,128)(2,1)S(1)} async-done(((bf16[128,16,512]{0,2,1:T(8,128)(2,1)}), bf16[128,16,512]{0,2,1:T(8,128)(2,1)S(1)}, u32[]{:S(2)}, u32[]{:S(2)}) %all-to-all-start) | async-done | bytes 2097184 | tf_op jit(solution)/shard_map/all_to_all | solution.py:38
  113.4 0.0 copy-start
  113.4 2.7 copy.13
  116.1 53.3 %all-gather.5.cloned.1.call-done = bf16[2048,512]{1,0:T(8,128)(2,1)} async-done(((bf16[128,512]{1,0:T(8,128)(2,1)}), bf16[2048,512]{1,0:T(8,128)(2,1)}) %all-gather.5.cloned.1.call-update) | async-done | bytes 2097168 | tf_op jit(solution)/shard_map/all_gather | solution.py:50
  169.4 0.0 copy-done
  169.4 3.5 fusion.5
  172.9 0.0 copy-start.1
  172.9 0.0 copy-start.2
  172.9 0.1 copy.15
  173.0 449.1 %all-reduce.2.cloned.1.call-done = bf16[512,128]{1,0:T(8,128)(2,1)} async-done(((bf16[512,128]{1,0:T(8,128)(2,1)}), bf16[512,128]{1,0:T(8,128)(2,1)}) %all-reduce.2.cloned.1.call-update) | async-done | bytes 131088 | tf_op jit(solution)/shard_map/psum | solution.py:58
  622.2 0.0 copy-done.1
  622.2 0.0 copy-done.2
  622.2 1.8 dynamic-slice_add_fusion
  624.0 2.2 mul.61
  626.2 1.0 fusion.12
  627.3 0.0 all-gather.3.cloned.1.call-done
  627.3 6.0 fusion.9
  (3 shorter events, 0.0 us)
Async XLA Ops:
  8.0 161.4 %all-gather.5.cloned.1.call-start = ((), (), s32[]{:S(2)}) async-start(), calls=%async_computation.2 | async-start | bytes 2228224 | tf_op jit(solution)/shard_map/all_gather | solution.py:50
  8.7 613.4 %all-reduce.2.cloned.1.call-start = ((), (), s32[]{:S(2)}) async-start(), calls=%async_computation.3 | async-start | bytes 262144 | tf_op jit(solution)/shard_map/psum | solution.py:58
  9.3 617.9 %all-gather.3.cloned.1.call-start = ((), (), s32[]{:S(2)}) async-start(), calls=%async_computation.1 | async-start | bytes 8912896 | tf_op jit(solution)/shard_map/all_gather | solution.py:42
  10.1 3.2 copy-start.3
  18.8 94.7 %all-to-all-start = ((bf16[128,16,512]{0,2,1:T(8,128)(2,1)}), bf16[128,16,512]{0,2,1:T(8,128)(2,1)S(1)}, u32[]{:S(2)}, u32[]{:S(2)}) async-start(bf16[128,16,512]{0,2,1:T(8,128)(2,1)} %bitcast.3), calls=%async_computation | async-start | bytes 4194304 | tf_op jit(solution)/shard_map/all_to_all | solution.py:38
  113.4 56.0 %copy-start = (bf16[1,512,512]{2,1,0:T(8,128)(2,1)S(1)}, bf16[1,512,512]{2,1,0:T(8,128)(2,1)}, u32[]{:S(2)}) copy-start(bf16[1,512,512]{2,1,0:T(8,128)(2,1)} %param.10) | copy-start | bytes 1572868
  172.9 449.2 %copy-start.1 = (f32[512,128]{1,0:T(8,128)S(1)}, f32[512,128]{1,0:T(8,128)}, u32[]{:S(2)}) copy-start(f32[512,128]{1,0:T(8,128)} %param.14) | copy-start | bytes 786436
  172.9 449.2 %copy-start.2 = (f32[512,128]{1,0:T(8,128)S(1)}, f32[512,128]{1,0:T(8,128)}, u32[]{:S(2)}) copy-start(f32[512,128]{1,0:T(8,128)} %param.15) | copy-start | bytes 786436
Sparse Core Ops, SparseCore 0:
  12.1 157.2 all-gather.4
  172.7 174.7 all-gather.2
Sparse Core Ops, SparseCore 1:
  12.1 610.0 all-reduce.1
where the time goes:
time: 641 us
  waiting for transfers between devices  580 us (90%)
  starting transfers between devices  18.3 us (3%)
  between operations  16.2 us (3%)
  matrix products  9.48 us (1%)
  other arithmetic  8.3 us (1%)
  local copies, waits for them, and re-layouts  8.21 us (1%)
    psum x1, waiting for transfers between devices, body(): lax.psum(pending_delta[0].astype(jnp.float32).astype(jnp.bfloat16), 'repl...  449 us
    all_to_all x1, waiting for transfers between devices, body(): lax.all_to_all(normed, 'fsdp', split_axis=1, concat_axis=0, tiled=True)  75.8 us
    all_gather x1, waiting for transfers between devices, body(): lax.all_gather(key_cotangent, 'fsdp', axis=0, tiled=True)  53.3 us
    all_to_all x1, starting transfers between devices, body(): lax.all_to_all(normed, 'fsdp', split_axis=1, concat_axis=0, tiled=True)  18.2 us
  transfers between devices with their start and end apart: 4, of which 3 were waited for; matrix products, arithmetic and copies ran while one was open for 3% of the time, Pallas kernels for 0%

commit v1 on v0

v1 whole, which is shorter than its diff:
```python
import jax
import jax.numpy as jnp
from jax import lax
from jax.experimental import pallas as pl
from jax.experimental.pallas import tpu as pltpu
from jax.sharding import PartitionSpec as P

D = 8192
HALF = 8
PARTS = 16
ROWS_IN = 128
BLOCK = 512
KVW = 512
INV_ROOT = D ** (-0.5)

inner_rate = 0.5
outer_rate = 0.7
momentum_coef = 0.9
blend_coef = 0.5

HALVES = [list(range(0, HALF)), list(range(HALF, PARTS))]
ALONG_X = [[x * 8 + z for x in range(4)] for z in range(8)]
ALONG_Z = [[x * 8 + z for z in range(8)] for x in range(4)]
ACROSS = [(f, f ^ HALF) for f in range(PARTS)]

TOK = 32


def norm_kernel(half_ref, acts_ref, gain_ref, cot_ref, far_ref, near_ref):
    half = half_ref[0]
    rows = acts_ref[...].astype(jnp.float32)
    scale = lax.rsqrt(jnp.mean(rows * rows, axis=-1, keepdims=True) + 1e-05)
    cot = cot_ref[...]
    span = HALF * BLOCK
    for j in range(HALF):
        for which, out in ((half, near_ref), (1 - half, far_ref)):
            at = pl.ds(pl.multiple_of(which * span + j * BLOCK, BLOCK), BLOCK)
            part = acts_ref[:, at].astype(jnp.float32) * scale * gain_ref[:, at].astype(jnp.float32)
            out[j, :, 0:BLOCK] = part.astype(jnp.bfloat16)
        far_ref[j, :, BLOCK : BLOCK + KVW] = cot


def normalise(half, acts, gain, cot):
    return pl.pallas_call(
        norm_kernel,
        grid_spec=pltpu.PrefetchScalarGridSpec(
            num_scalar_prefetch=1,
            grid=(ROWS_IN // TOK,),
            in_specs=[
                pl.BlockSpec((TOK, D), lambda i, h: (i, 0)),
                pl.BlockSpec((1, D), lambda i, h: (0, 0)),
                pl.BlockSpec((TOK, KVW), lambda i, h: (i, 0)),
            ],
            out_specs=[
                pl.BlockSpec((HALF, TOK, BLOCK + KVW), lambda i, h: (0, i, 0)),
                pl.BlockSpec((HALF, TOK, BLOCK), lambda i, h: (0, i, 0)),
            ],
        ),
        out_shape=[
            jax.ShapeDtypeStruct((HALF, ROWS_IN, BLOCK + KVW), jnp.bfloat16),
            jax.ShapeDtypeStruct((HALF, ROWS_IN, BLOCK), jnp.bfloat16),
        ],
        compiler_params=pltpu.CompilerParams(vmem_limit_bytes=32 * 1024 * 1024),
        name="normalise",
    )(half, acts, gain, cot)


def transposed_dot(left, right):
    return lax.dot_general(left, right, (((0,), (0,)), ((), ())), preferred_element_type=jnp.float32)


def far_kernel(normed_ref, cot_ref, out_ref):
    out_ref[...] = (transposed_dot(normed_ref[...], cot_ref[...]) * INV_ROOT).astype(jnp.bfloat16)


def far_gradient(far):
    tokens = far.shape[0]
    step = 256
    return pl.pallas_call(
        far_kernel,
        grid=(BLOCK // step,),
        in_specs=[
            pl.BlockSpec((tokens, step), lambda i: (0, i)),
            pl.BlockSpec((tokens, KVW), lambda i: (0, BLOCK // KVW)),
        ],
        out_specs=pl.BlockSpec((step, KVW), lambda i: (i, 0)),
        out_shape=jax.ShapeDtypeStruct((BLOCK, KVW), jnp.bfloat16),
        compiler_params=pltpu.CompilerParams(vmem_limit_bytes=32 * 1024 * 1024),
        name="far_gradient",
    )(far, far)


def near_kernel(far_ref, near_ref, near_weight_ref, far_weight_ref, keys_ref, stepped_ref):
    near = near_ref[...]
    keys = jnp.dot(near, near_weight_ref[...], preferred_element_type=jnp.float32)
    keys += jnp.dot(far_ref[:, 0:BLOCK], far_weight_ref[...], preferred_element_type=jnp.float32)
    keys_ref[...] = (keys * INV_ROOT).astype(jnp.bfloat16)
    gradient = transposed_dot(near, far_ref[:, BLOCK : BLOCK + KVW]) * INV_ROOT
    stepped_ref[...] = near_weight_ref[...].astype(jnp.float32) - inner_rate * gradient


def near_work(far, near, near_weight, far_weight):
    tokens = far.shape[0]
    return pl.pallas_call(
        near_kernel,
        out_shape=[
            jax.ShapeDtypeStruct((tokens, KVW), jnp.bfloat16),
            jax.ShapeDtypeStruct((BLOCK, KVW), jnp.float32),
        ],
        in_specs=[pl.BlockSpec(memory_space=pltpu.VMEM)] * 4,
        out_specs=[pl.BlockSpec(memory_space=pltpu.VMEM)] * 2,
        compiler_params=pltpu.CompilerParams(vmem_limit_bytes=48 * 1024 * 1024),
        name="near_work",
    )(far, near, near_weight, far_weight)


def exchange(rows, axis, groups):
    return lax.all_to_all(rows, axis, split_axis=0, concat_axis=0, tiled=True, axis_index_groups=groups)


def sum_parts(rows, parts):
    stacked = rows.reshape(parts, rows.shape[0] // parts, rows.shape[1])
    return jnp.sum(stacked.astype(jnp.float32), axis=0)


def delta_sum(delta):
    along_x = sum_parts(exchange(delta, "replica", ALONG_X), 4).astype(jnp.bfloat16)
    total = sum_parts(exchange(along_x, "replica", ALONG_Z), 8).astype(jnp.bfloat16)
    spread_z = exchange(jnp.tile(total, (8, 1)), "replica", ALONG_Z)
    return exchange(jnp.tile(spread_z, (4, 1)), "replica", ALONG_X).astype(jnp.float32)


def place_fragment(global_new, start, kv_width):
    placed = jnp.zeros((global_new.shape[0], kv_width), global_new.dtype)
    placed = lax.dynamic_update_slice(placed, global_new, (jnp.zeros((), jnp.int32), start))
    column = lax.broadcasted_iota(jnp.int32, (1, kv_width), 1) - start
    inside = (column >= 0) & (column < global_new.shape[1])
    return (placed, inside)


def body(
    acts,
    norm_gain,
    key_weight,
    key_cotangent,
    pending_delta,
    fragment_index,
    global_frag,
    outer_mom,
):
    weight = key_weight[0]
    far_weight = lax.ppermute(weight, "fsdp", ACROSS)
    half = (lax.axis_index("fsdp") // HALF).astype(jnp.int32).reshape(1)
    far, near = normalise(half, acts, norm_gain.reshape(1, D), key_cotangent)

    far = exchange(far.reshape(HALF * ROWS_IN, BLOCK + KVW), "fsdp", HALVES)
    sent = far_gradient(far)
    arrived = lax.ppermute(sent, "fsdp", ACROSS)

    near, _ = lax.optimization_barrier((near, sent))
    near = exchange(near.reshape(HALF * ROWS_IN, BLOCK), "fsdp", HALVES)
    keys, stepped = near_work(far, near, weight, far_weight)
    key_out = sum_parts(exchange(keys, "fsdp", HALVES), HALF).astype(jnp.bfloat16)

    replicas = lax.axis_size("replica")
    mean_delta = delta_sum(pending_delta[0]) / replicas
    mom_new = momentum_coef * outer_mom + mean_delta
    global_new = global_frag - outer_rate * (momentum_coef * mom_new + mean_delta)
    placed, in_fragment = place_fragment(global_new, fragment_index[0], KVW)

    stepped, placed = lax.optimization_barrier((stepped, placed))
    stepped = stepped - inner_rate * arrived.astype(jnp.float32)
    blended = jnp.where(in_fragment, blend_coef * stepped + (1.0 - blend_coef) * placed, stepped)
    new_weight = blended.astype(jnp.bfloat16)[None]
    return (key_out, new_weight, global_new, mom_new)


def solution(mesh):
    in_specs = (
        P(("replica", "fsdp"), None),
        P(),
        P("replica", "fsdp", None),
        P(("replica", "fsdp"), None),
        P("replica", "fsdp", None),
        P(),
        P("fsdp", None),
        P("fsdp", None),
    )
    out_specs = (
        P(("replica", "fsdp"), None),
        P("replica", "fsdp", None),
        P("fsdp", None),
        P("fsdp", None),
    )
    return jax.shard_map(body, mesh=mesh, in_specs=in_specs, out_specs=out_specs, check_vma=False)
```

time: 641 us -> 200 us (0.31)
  the two profiles are of different devices: /device:TPU:8 before, /device:TPU:41 now
where the time goes in v1:
time: 200 us; the launch traced here: 199 us
  waiting for transfers between devices  107 us (54%)
  starting transfers between devices  58.7 us (29%)
  local copies, waits for them, and re-layouts  11 us (6%)
  blocking collectives  8.85 us (4%)
  Pallas kernels  7.44 us (4%)
  other arithmetic  4.71 us (2%)
    all_to_all x6, starting transfers between devices, exchange(): lax.all_to_all(rows, axis, split_axis=0, concat_axis=0, tiled=True, axis_...  42.9 us
    ppermute x1, waiting for transfers between devices, body(): far_weight = lax.ppermute(weight, 'fsdp', ACROSS)  40.2 us
    all_to_all x6, waiting for transfers between devices, exchange(): lax.all_to_all(rows, axis, split_axis=0, concat_axis=0, tiled=True, axis_...  39.5 us
    ppermute x1, waiting for transfers between devices, body(): arrived = lax.ppermute(sent, 'fsdp', ACROSS)  27.1 us
    all_to_all x1, blocking collectives, exchange(): lax.all_to_all(rows, axis, split_axis=0, concat_axis=0, tiled=True, axis_...  8.85 us
    ppermute x1, starting transfers between devices, body(): arrived = lax.ppermute(sent, 'fsdp', ACROSS)  7.94 us
    ppermute x1, starting transfers between devices, body(): far_weight = lax.ppermute(weight, 'fsdp', ACROSS)  7.93 us
    unnamed x20, local copies, waits for them, and re-layouts  5.68 us
  transfers between devices with their start and end apart: 8, of which 6 were waited for; matrix products, arithmetic and copies ran while one was open for 4% of the time, Pallas kernels for 4%

profile of v1, /device:TPU:41, one launch (start us, length us, event | category | flops | bytes accessed | tf_op | source)
XLA Modules:
  0.0 199.0 jit_solution(13931148162034387008)
XLA Ops:
  0.6 8.9 %all_to_all.55 = bf16[4,128,128]{2,1,0:T(8,128)(2,1)S(1)} all-to-all(bf16[4,128,128]{2,1,0:T(8,128)(2,1)} %bitcast.30), channel_id=1, replica_groups={{0,128,256,384},{16,144,272,400},{32,160,288,416},{48,176,304,432},{64,..., dimensions={0} | all-to-all | bytes 262144 | tf_op jit(solution)/shard_map/all_to_all | solution.py:118
  9.5 0.6 reduce_sum.37
  10.1 12.1 %all-to-all-start.4 = ((bf16[8,16,128]{2,1,0:T(8,128)(2,1)}), bf16[8,16,128]{2,1,0:T(8,128)(2,1)S(1)}, u32[]{:S(2)}, u32[]{:S(2)}) async-start(bf16[8,16,128]{2,1,0:T(8,128)(2,1)} %bitcast.7), calls=%async_computation.4 | async-start | bytes 65536 | tf_op jit(solution)/shard_map/all_to_all | solution.py:118
  22.2 0.7 reshape.65.gain_ref
  23.0 1.6 copy-done.1
  24.5 0.9 copy-done.6
  25.4 2.4 %normalise.1 = (bf16[8,128,1024]{2,1,0:T(8,128)(2,1)S(1)}, bf16[8,128,512]{2,1,0:T(8,128)(2,1)}) custom-call(s32[1]{0:T(128)} %bitcast.half_ref, bf16[128,8192]{1,0:T(8,128)(2,1)S(1)} %copy-done.1, bf16[1,8192]{1,0:T(2,128)(2,1)S(1)} %reshape.65.gain_ref, bf16[128,512]{1,0:T(8,128)(2,1)S(1)} %copy-done.6), custom_call_target="tpu_custom_call" | custom-call | tf_op jit(solution)/shard_map/normalise/pallas_call | solution.py:44
  27.9 1.3 copy-done.2
  29.2 1.2 all-to-all-done.4
  30.4 8.1 %all-to-all-start = ((bf16[8,128,1024]{2,1,0:T(8,128)(2,1)}), bf16[8,128,1024]{2,1,0:T(8,128)(2,1)S(1)}, u32[]{:S(2)}, u32[]{:S(2)}) async-start(bf16[8,128,1024]{2,1,0:T(8,128)(2,1)} %copy-done.2), calls=%async_computation | async-start | bytes 4194304 | tf_op jit(solution)/shard_map/all_to_all | solution.py:118
  38.5 25.2 %all-to-all-done = bf16[8,128,1024]{2,1,0:T(8,128)(2,1)S(1)} async-done(((bf16[8,128,1024]{2,1,0:T(8,128)(2,1)}), bf16[8,128,1024]{2,1,0:T(8,128)(2,1)S(1)}, u32[]{:S(2)}, u32[]{:S(2)}) %all-to-all-start) | async-done | bytes 2097184 | tf_op jit(solution)/shard_map/all_to_all | solution.py:118
  63.7 0.7 tile.6
  64.4 7.3 %all-to-all-start.5 = ((bf16[8,16,128]{2,1,0:T(8,128)(2,1)}), bf16[8,16,128]{2,1,0:T(8,128)(2,1)S(1)}, u32[]{:S(2)}, u32[]{:S(2)}) async-start(bf16[8,16,128]{2,1,0:T(8,128)(2,1)} %tile.6), calls=%async_computation.5 | async-start | bytes 65536 | tf_op jit(solution)/shard_map/all_to_all | solution.py:118
  71.7 1.2 far_gradient.1
  72.9 7.0 %all-to-all-done.5 = bf16[8,16,128]{2,1,0:T(8,128)(2,1)S(1)} async-done(((bf16[8,16,128]{2,1,0:T(8,128)(2,1)}), bf16[8,16,128]{2,1,0:T(8,128)(2,1)S(1)}, u32[]{:S(2)}, u32[]{:S(2)}) %all-to-all-start.5) | async-done | bytes 32800 | tf_op jit(solution)/shard_map/all_to_all | solution.py:118
  79.9 6.9 %all-to-all-start.1 = ((bf16[8,128,512]{2,1,0:T(8,128)(2,1)}), bf16[8,128,512]{2,1,0:T(8,128)(2,1)S(1)}, u32[]{:S(2)}, u32[]{:S(2)}) async-start(bf16[8,128,512]{2,1,0:T(8,128)(2,1)} %get-tuple-element.13), calls=%async_computation.1 | async-start | bytes 2097152 | tf_op jit(solution)/shard_map/all_to_all | solution.py:118
  86.8 7.9 %collective-permute-start = (bf16[512,512]{1,0:T(8,128)(2,1)S(1)}, bf16[512,512]{1,0:T(8,128)(2,1)S(1)}, u32[]{:S(2)}, u32[]{:S(2)}) collective-permute-start(bf16[512,512]{1,0:T(8,128)(2,1)S(1)} %bitcast.27), channel_id=1, source_target_pairs={{0,8},{1,9},{2,10},{3,11},{4,12},{5,13},{6,14},{7,15},{8,0},{9,1},... | collective-permute-start | bytes 1572872 | tf_op jit(solution)/shard_map/ppermute | solution.py:152
  94.7 6.1 %all-to-all-done.1 = bf16[8,128,512]{2,1,0:T(8,128)(2,1)S(1)} async-done(((bf16[8,128,512]{2,1,0:T(8,128)(2,1)}), bf16[8,128,512]{2,1,0:T(8,128)(2,1)S(1)}, u32[]{:S(2)}, u32[]{:S(2)}) %all-to-all-start.1) | async-done | bytes 1048608 | tf_op jit(solution)/shard_map/all_to_all | solution.py:118
  100.8 0.7 tile.8
  101.5 3.3 %all-to-all-start.6 = ((bf16[4,128,128]{2,1,0:T(8,128)(2,1)}), bf16[4,128,128]{2,1,0:T(8,128)(2,1)S(1)}, u32[]{:S(2)}, u32[]{:S(2)}) async-start(bf16[4,128,128]{2,1,0:T(8,128)(2,1)} %tile.8), calls=%async_computation.6 | async-start | bytes 262144 | tf_op jit(solution)/shard_map/all_to_all | solution.py:118
  104.8 40.2 %collective-permute-done.far_weight_ref = bf16[512,512]{1,0:T(8,128)(2,1)S(1)} collective-permute-done((bf16[512,512]{1,0:T(8,128)(2,1)S(1)}, bf16[512,512]{1,0:T(8,128)(2,1)S(1)}, u32[]{:S(2)}, u32[]{:S(2)}) %collective-permute-start) | collective-permute-done | bytes 524320 | tf_op jit(solution)/shard_map/ppermute | solution.py:152
  145.1 0.8 copy-done.4
  145.9 1.0 copy-done.5
  146.9 3.8 %near_work.1 = (bf16[1024,512]{1,0:T(8,128)(2,1)}, f32[512,512]{1,0:T(8,128)S(1)}) custom-call(bf16[1024,1024]{1,0:T(8,128)(2,1)} %bitcast.25, bf16[1024,512]{1,0:T(8,128)(2,1)S(1)} %bitcast.26, bf16[512,512]{1,0:T(8,128)(2,1)S(1)} %bitcast.28, bf16[512,512]{1,0:T(8,128)(2,1)S(1)} %copy-done.5), custom_call_target="tpu_custom_call" | custom-call | tf_op jit(solution)/shard_map/near_work/pallas_call | solution.py:104
  150.7 5.2 %all-to-all-start.2 = ((bf16[8,128,512]{2,1,0:T(8,128)(2,1)}), bf16[8,128,512]{2,1,0:T(8,128)(2,1)S(1)}, u32[]{:S(2)}, u32[]{:S(2)}) async-start(bf16[8,128,512]{2,1,0:T(8,128)(2,1)} %bitcast.4), calls=%async_computation.2 | async-start | bytes 2097152 | tf_op jit(solution)/shard_map/all_to_all | solution.py:118
  156.6 7.9 %collective-permute-start.1 = (bf16[512,512]{1,0:T(8,128)(2,1)S(1)}, bf16[512,512]{1,0:T(8,128)(2,1)}, u32[]{:S(2)}, u32[]{:S(2)}) collective-permute-start(bf16[512,512]{1,0:T(8,128)(2,1)S(1)} %far_gradient.1), channel_id=1, source_target_pairs={{0,8},{1,9},{2,10},{3,11},{4,12},{5,13},{6,14},{7,15},{8,0},{9,1},... | collective-permute-start | bytes 1572872 | tf_op jit(solution)/shard_map/ppermute | solution.py:158
  164.6 0.8 fusion.2
  165.4 1.1 broadcast_in_dim.15
  166.5 2.2 %dynamic_update_slice.3 = f32[512,512]{1,0:T(8,128)} dynamic-update-slice(f32[512,512]{1,0:T(8,128)} %broadcast_in_dim.15, f32[512,128]{1,0:T(8,128)S(1)} %get-tuple-element.18, s32[]{:T(128)} %constant.30.clone.1, s32[]{:T(128)S(6)} %select_n.13) | dynamic-update-slice | bytes 524292 | tf_op jit(solution)/shard_map/dynamic_update_slice | solution.py:135
  168.6 27.1 %collective-permute-done.1 = bf16[512,512]{1,0:T(8,128)(2,1)} collective-permute-done((bf16[512,512]{1,0:T(8,128)(2,1)S(1)}, bf16[512,512]{1,0:T(8,128)(2,1)}, u32[]{:S(2)}, u32[]{:S(2)}) %collective-permute-start.1) | collective-permute-done | bytes 524320 | tf_op jit(solution)/shard_map/ppermute | solution.py:158
  195.7 2.5 %fusion = bf16[1,512,512]{2,1,0:T(8,128)(2,1)} fusion(f32[512,512]{1,0:T(8,128)} %dynamic_update_slice.3, f32[512,512]{1,0:T(8,128)S(1)} %get-tuple-element.16, bf16[512,512]{1,0:T(8,128)(2,1)} %collective-permute-done.1, pred[512]{0:T(512)(128)(4,1)S(1)} %fusion.5), kind=kLoop, calls=%fused_computation.1 | loop fusion | flops 1835008 | bytes 3146240 | tf_op jit(solution)/shard_map/broadcast_in_dim | solution.py:174
  198.2 0.8 reduce_sum.36
  (20 shorter events, 0.1 us)
Async XLA Ops:
  10.1 20.3 %all-to-all-start.4 = ((bf16[8,16,128]{2,1,0:T(8,128)(2,1)}), bf16[8,16,128]{2,1,0:T(8,128)(2,1)S(1)}, u32[]{:S(2)}, u32[]{:S(2)}) async-start(bf16[8,16,128]{2,1,0:T(8,128)(2,1)} %bitcast.7), calls=%async_computation.4 | async-start | bytes 65536 | tf_op jit(solution)/shard_map/all_to_all | solution.py:118
  22.9 1.6 copy-start.1
  24.5 0.9 copy-start.6
  27.9 1.3 copy-start.2
  30.4 33.3 %all-to-all-start = ((bf16[8,128,1024]{2,1,0:T(8,128)(2,1)}), bf16[8,128,1024]{2,1,0:T(8,128)(2,1)S(1)}, u32[]{:S(2)}, u32[]{:S(2)}) async-start(bf16[8,128,1024]{2,1,0:T(8,128)(2,1)} %copy-done.2), calls=%async_computation | async-start | bytes 4194304 | tf_op jit(solution)/shard_map/all_to_all | solution.py:118
  63.7 9.2 %copy-start = (bf16[8,128,1024]{2,1,0:T(8,128)(2,1)}, bf16[8,128,1024]{2,1,0:T(8,128)(2,1)S(1)}, u32[]{:S(2)}) copy-start(bf16[8,128,1024]{2,1,0:T(8,128)(2,1)S(1)} %all-to-all-done) | copy-start | bytes 6291460
  64.4 15.5 %all-to-all-start.5 = ((bf16[8,16,128]{2,1,0:T(8,128)(2,1)}), bf16[8,16,128]{2,1,0:T(8,128)(2,1)S(1)}, u32[]{:S(2)}, u32[]{:S(2)}) async-start(bf16[8,16,128]{2,1,0:T(8,128)(2,1)} %tile.6), calls=%async_computation.5 | async-start | bytes 65536 | tf_op jit(solution)/shard_map/all_to_all | solution.py:118
  72.9 13.9 %copy-start.3 = (bf16[1,512,512]{2,1,0:T(8,128)(2,1)S(1)}, bf16[1,512,512]{2,1,0:T(8,128)(2,1)}, u32[]{:S(2)}) copy-start(bf16[1,512,512]{2,1,0:T(8,128)(2,1)} %param.10) | copy-start | bytes 1572868
  79.9 20.9 %all-to-all-start.1 = ((bf16[8,128,512]{2,1,0:T(8,128)(2,1)}), bf16[8,128,512]{2,1,0:T(8,128)(2,1)S(1)}, u32[]{:S(2)}, u32[]{:S(2)}) async-start(bf16[8,128,512]{2,1,0:T(8,128)(2,1)} %get-tuple-element.13), calls=%async_computation.1 | async-start | bytes 2097152 | tf_op jit(solution)/shard_map/all_to_all | solution.py:118
  86.8 58.3 %collective-permute-start = (bf16[512,512]{1,0:T(8,128)(2,1)S(1)}, bf16[512,512]{1,0:T(8,128)(2,1)S(1)}, u32[]{:S(2)}, u32[]{:S(2)}) collective-permute-start(bf16[512,512]{1,0:T(8,128)(2,1)S(1)} %bitcast.27), channel_id=1, source_target_pairs={{0,8},{1,9},{2,10},{3,11},{4,12},{5,13},{6,14},{7,15},{8,0},{9,1},... | collective-permute-start | bytes 1572872 | tf_op jit(solution)/shard_map/ppermute | solution.py:152
  101.5 49.2 %all-to-all-start.6 = ((bf16[4,128,128]{2,1,0:T(8,128)(2,1)}), bf16[4,128,128]{2,1,0:T(8,128)(2,1)S(1)}, u32[]{:S(2)}, u32[]{:S(2)}) async-start(bf16[4,128,128]{2,1,0:T(8,128)(2,1)} %tile.8), calls=%async_computation.6 | async-start | bytes 262144 | tf_op jit(solution)/shard_map/all_to_all | solution.py:118
  145.1 0.8 copy-start.4
  145.9 1.0 copy-start.5
  150.7 13.9 %copy-start.8 = (f32[512,128]{1,0:T(8,128)S(1)}, f32[512,128]{1,0:T(8,128)}, u32[]{:S(2)}) copy-start(f32[512,128]{1,0:T(8,128)} %param.14) | copy-start | bytes 786436
  150.7 13.9 %copy-start.9 = (f32[512,128]{1,0:T(8,128)S(1)}, f32[512,128]{1,0:T(8,128)}, u32[]{:S(2)}) copy-start(f32[512,128]{1,0:T(8,128)} %param.15) | copy-start | bytes 786436
  150.7 47.5 %all-to-all-start.2 = ((bf16[8,128,512]{2,1,0:T(8,128)(2,1)}), bf16[8,128,512]{2,1,0:T(8,128)(2,1)S(1)}, u32[]{:S(2)}, u32[]{:S(2)}) async-start(bf16[8,128,512]{2,1,0:T(8,128)(2,1)} %bitcast.4), calls=%async_computation.2 | async-start | bytes 2097152 | tf_op jit(solution)/shard_map/all_to_all | solution.py:118
  156.6 39.1 %collective-permute-start.1 = (bf16[512,512]{1,0:T(8,128)(2,1)S(1)}, bf16[512,512]{1,0:T(8,128)(2,1)}, u32[]{:S(2)}, u32[]{:S(2)}) collective-permute-start(bf16[512,512]{1,0:T(8,128)(2,1)S(1)} %far_gradient.1), channel_id=1, source_target_pairs={{0,8},{1,9},{2,10},{3,11},{4,12},{5,13},{6,14},{7,15},{8,0},{9,1},... | collective-permute-start | bytes 1572872 | tf_op jit(solution)/shard_map/ppermute | solution.py:158
  165.4 32.8 %copy-start.7 = (f32[512,128]{1,0:T(8,128)}, f32[512,128]{1,0:T(8,128)S(1)}, u32[]{:S(2)}) copy-start(f32[512,128]{1,0:T(8,128)S(1)} %get-tuple-element.18) | copy-start | bytes 786436

commit v2 on v1

v2 whole, which is shorter than its diff:
```python
import jax
import jax.numpy as jnp
from jax import lax
from jax.experimental import pallas as pl
from jax.experimental.pallas import tpu as pltpu
from jax.sharding import PartitionSpec as P

D = 8192
HALF = 8
PARTS = 16
ROWS_IN = 128
BLOCK = 512
KVW = 512
HD = 128
REPLICAS = 32
INV_ROOT = D ** (-0.5)

inner_rate = 0.5
outer_rate = 0.7
momentum_coef = 0.9
blend_coef = 0.5

HALVES = [list(range(0, HALF)), list(range(HALF, PARTS))]
ALONG_X = [[x * 8 + z for x in range(4)] for z in range(8)]
ALONG_Z = [[x * 8 + z for z in range(8)] for x in range(4)]
ACROSS = [(f, f ^ HALF) for f in range(PARTS)]

TOK = 32
NEAR = 0
FAR = BLOCK
COT = 2 * BLOCK
WIDE = 2 * BLOCK + KVW


def norm_kernel(half_ref, acts_ref, gain_ref, cot_ref, out_ref):
    half = half_ref[0]
    rows = acts_ref[...].astype(jnp.float32)
    scale = lax.rsqrt(jnp.mean(rows * rows, axis=-1, keepdims=True) + 1e-05)
    cot = cot_ref[...]
    span = HALF * BLOCK
    for j in range(HALF):
        for which, slot in ((half, NEAR), (1 - half, FAR)):
            at = pl.ds(pl.multiple_of(which * span + j * BLOCK, BLOCK), BLOCK)
            part = acts_ref[:, at].astype(jnp.float32) * scale * gain_ref[:, at].astype(jnp.float32)
            out_ref[j, :, slot : slot + BLOCK] = part.astype(jnp.bfloat16)
        out_ref[j, :, COT : COT + KVW] = cot


def normalise(half, acts, gain, cot):
    return pl.pallas_call(
        norm_kernel,
        grid_spec=pltpu.PrefetchScalarGridSpec(
            num_scalar_prefetch=1,
            grid=(ROWS_IN // TOK,),
            in_specs=[
                pl.BlockSpec((TOK, D), lambda i, h: (i, 0)),
                pl.BlockSpec((1, D), lambda i, h: (0, 0)),
                pl.BlockSpec((TOK, KVW), lambda i, h: (i, 0)),
            ],
            out_specs=pl.BlockSpec((HALF, TOK, WIDE), lambda i, h: (0, i, 0)),
        ),
        out_shape=jax.ShapeDtypeStruct((HALF, ROWS_IN, WIDE), jnp.bfloat16),
        compiler_params=pltpu.CompilerParams(vmem_limit_bytes=32 * 1024 * 1024),
        name="normalise",
    )(half, acts, gain, cot)


def transposed_dot(left, right):
    return lax.dot_general(left, right, (((0,), (0,)), ((), ())), preferred_element_type=jnp.float32)


def far_kernel(normed_ref, cot_ref, out_ref):
    out_ref[...] = (transposed_dot(normed_ref[...], cot_ref[...]) * INV_ROOT).astype(jnp.bfloat16)


def far_gradient(mixed):
    tokens = mixed.shape[0]
    step = 256
    return pl.pallas_call(
        far_kernel,
        grid=(BLOCK // step,),
        in_specs=[
            pl.BlockSpec((tokens, step), lambda i: (0, FAR // step + i)),
            pl.BlockSpec((tokens, KVW), lambda i: (0, COT // KVW)),
        ],
        out_specs=pl.BlockSpec((step, KVW), lambda i: (i, 0)),
        out_shape=jax.ShapeDtypeStruct((BLOCK, KVW), jnp.bfloat16),
        compiler_params=pltpu.CompilerParams(vmem_limit_bytes=32 * 1024 * 1024),
        name="far_gradient",
    )(mixed, mixed)


def near_kernel(mixed_ref, near_weight_ref, far_weight_ref, keys_ref, stepped_ref):
    near = mixed_ref[:, NEAR : NEAR + BLOCK]
    keys = jnp.dot(near, near_weight_ref[...], preferred_element_type=jnp.float32)
    keys += jnp.dot(mixed_ref[:, FAR : FAR + BLOCK], far_weight_ref[...], preferred_element_type=jnp.float32)
    keys_ref[...] = (keys * INV_ROOT).astype(jnp.bfloat16)
    gradient = transposed_dot(near, mixed_ref[:, COT : COT + KVW]) * INV_ROOT
    stepped_ref[...] = near_weight_ref[...].astype(jnp.float32) - inner_rate * gradient


def near_work(mixed, near_weight, far_weight):
    tokens = mixed.shape[0]
    return pl.pallas_call(
        near_kernel,
        out_shape=[
            jax.ShapeDtypeStruct((tokens, KVW), jnp.bfloat16),
            jax.ShapeDtypeStruct((BLOCK, KVW), jnp.float32),
        ],
        in_specs=[pl.BlockSpec(memory_space=pltpu.VMEM)] * 3,
        out_specs=[pl.BlockSpec(memory_space=pltpu.VMEM)] * 2,
        compiler_params=pltpu.CompilerParams(vmem_limit_bytes=48 * 1024 * 1024),
        name="near_work",
    )(mixed, near_weight, far_weight)


def blend_kernel(start_ref, stepped_ref, arrived_ref, ours_ref, theirs_ref, frag_ref, mom_ref, out_ref, global_ref, mom_new_ref):
    start = start_ref[0]
    mean = (ours_ref[...].astype(jnp.float32) + theirs_ref[...].astype(jnp.float32)) * (1.0 / REPLICAS)
    mom_new = momentum_coef * mom_ref[...] + mean
    global_new = frag_ref[...] - outer_rate * (momentum_coef * mom_new + mean)
    mom_new_ref[...] = mom_new
    global_ref[...] = global_new
    stepped = stepped_ref[...] - inner_rate * arrived_ref[...].astype(jnp.float32)
    wide = jnp.concatenate([global_new, jnp.zeros((global_new.shape[0], KVW - HD), jnp.float32)], axis=1)
    placed = pltpu.roll(wide, start, 1)
    column = lax.broadcasted_iota(jnp.int32, placed.shape, 1) - start
    inside = (column >= 0) & (column < HD)
    blended = jnp.where(inside, blend_coef * stepped + (1.0 - blend_coef) * placed, stepped)
    out_ref[...] = blended.astype(jnp.bfloat16)


def blend(start, stepped, arrived, ours, theirs, frag, mom):
    step = 128
    wide = pl.BlockSpec((step, KVW), lambda i, s: (i, 0))
    slim = pl.BlockSpec((step, HD), lambda i, s: (i, 0))
    return pl.pallas_call(
        blend_kernel,
        grid_spec=pltpu.PrefetchScalarGridSpec(
            num_scalar_prefetch=1,
            grid=(BLOCK // step,),
            in_specs=[wide, wide, slim, slim, slim, slim],
            out_specs=[wide, slim, slim],
        ),
        out_shape=[
            jax.ShapeDtypeStruct((BLOCK, KVW), jnp.bfloat16),
            jax.ShapeDtypeStruct((BLOCK, HD), jnp.float32),
            jax.ShapeDtypeStruct((BLOCK, HD), jnp.float32),
        ],
        compiler_params=pltpu.CompilerParams(vmem_limit_bytes=32 * 1024 * 1024),
        name="blend",
    )(start, stepped, arrived, ours, theirs, frag, mom)


def staged(go, work, *operands):
    shapes = jax.eval_shape(work, *operands)
    skip = lambda *_: jax.tree.map(lambda leaf: jnp.zeros(leaf.shape, leaf.dtype), shapes)
    return lax.cond(go, work, skip, *operands)


def exchange(rows, axis, groups):
    return lax.all_to_all(rows, axis, split_axis=0, concat_axis=0, tiled=True, axis_index_groups=groups)


def sum_parts(rows, parts):
    stacked = rows.reshape(parts, rows.shape[0] // parts, rows.shape[1])
    return jnp.sum(stacked.astype(jnp.float32), axis=0)


def turned(rows, by):
    ring = [(x * 8 + z, ((x + by) % 4) * 8 + z) for x in range(4) for z in range(8)]
    return lax.ppermute(rows, "replica", ring)


def paired(rows, bits):
    return lax.ppermute(rows, "replica", [(r, r ^ bits) for r in range(REPLICAS)])


def own_x():
    return lax.axis_index("replica") // 8


def reduce_x(delta):
    part = delta.shape[0] // 4
    x = own_x()
    pick = lambda by: lax.dynamic_slice_in_dim(delta, lax.rem(x + by, 4) * part, part)
    total = pick(0).astype(jnp.float32)
    for arrived in [turned(pick(by), by) for by in range(1, 4)]:
        total += arrived.astype(jnp.float32)
    return total.astype(jnp.bfloat16)


def spread_x(total):
    blocks = [total] + [turned(total, by) for by in range(1, 4)]
    x = own_x()
    out = jnp.zeros((4 * total.shape[0], total.shape[1]), total.dtype)
    for by in range(4):
        at = lax.rem(x + 4 - by, 4) * total.shape[0]
        out = lax.dynamic_update_slice_in_dim(out, blocks[by], at, 0)
    return out


def body(
    acts,
    norm_gain,
    key_weight,
    key_cotangent,
    pending_delta,
    fragment_index,
    global_frag,
    outer_mom,
):
    weight = key_weight[0]
    go = fragment_index[0] >= 0
    far_weight = lax.ppermute(weight, "fsdp", ACROSS)

    def first(acts, gain, cot, delta):
        half = (lax.axis_index("fsdp") // HALF).astype(jnp.int32).reshape(1)
        mixed = normalise(half, acts, gain.reshape(1, D), cot)
        delta, mixed = lax.optimization_barrier((delta, mixed))
        mixed = exchange(mixed.reshape(HALF * ROWS_IN, WIDE), "fsdp", HALVES)
        own = staged(go, reduce_x, delta)
        arrivals = [paired(own, bits) for bits in (2, 4, 6)]
        sent = far_gradient(mixed)
        arrivals, own, sent = lax.optimization_barrier((arrivals, own, sent))
        total = own.astype(jnp.float32)
        for arrived in arrivals:
            total += arrived.astype(jnp.float32)
        return mixed, total.astype(jnp.bfloat16), sent

    mixed, some, sent = staged(go, first, acts, norm_gain, key_cotangent, pending_delta[0])
    arrived = lax.ppermute(sent, "fsdp", ACROSS)

    def second(mixed, some, weight, far_weight):
        keys, stepped = near_work(mixed, weight, far_weight)
        return keys, stepped, spread_x(some)

    keys, stepped, ours = staged(go, second, mixed, some, weight, far_weight)
    theirs = paired(ours, 1)

    def third(keys):
        return sum_parts(exchange(keys, "fsdp", HALVES), HALF).astype(jnp.bfloat16)

    key_out = staged(go, third, keys)
    key_out, arrived, theirs = lax.optimization_barrier((key_out, arrived, theirs))
    new_weight, global_new, mom_new = blend(fragment_index, stepped, arrived, ours, theirs, global_frag, outer_mom)
    return (key_out, new_weight[None], global_new, mom_new)


def solution(mesh):
    in_specs = (
        P(("replica", "fsdp"), None),
        P(),
        P("replica", "fsdp", None),
        P(("replica", "fsdp"), None),
        P("replica", "fsdp", None),
        P(),
        P("fsdp", None),
        P("fsdp", None),
    )
    out_specs = (
        P(("replica", "fsdp"), None),
        P("replica", "fsdp", None),
        P("fsdp", None),
        P("fsdp", None),
    )
    return jax.shard_map(body, mesh=mesh, in_specs=in_specs, out_specs=out_specs, check_vma=False)
```

time: 200 us -> 130 us (0.65)
  the two profiles are of different devices: /device:TPU:41 before, /device:TPU:20 now
where the time goes in v2:
time: 130 us; the launch traced here: 129 us
  starting transfers between devices  61.8 us (48%)
  waiting for transfers between devices  28.2 us (22%)
  blocking collectives  17.6 us (14%)
  Pallas kernels  14.6 us (11%)
  local copies, waits for them, and re-layouts  3.94 us (3%)
  other arithmetic  1.42 us (1%)
  between operations  1.35 us (1%)
    ppermute x4, starting transfers between devices, paired(): lax.ppermute(rows, 'replica', [(r, r ^ bits) for r in range(REPLICAS)])  19.6 us
    ppermute x6, starting transfers between devices, turned(): return lax.ppermute(rows, 'replica', ring)  18.5 us
    all_to_all x1, blocking collectives, exchange(): lax.all_to_all(rows, axis, split_axis=0, concat_axis=0, tiled=True, axis_...  17.6 us
    ppermute x1, starting transfers between devices, body(): far_weight = lax.ppermute(weight, 'fsdp', ACROSS)  15.7 us
    ppermute x1, waiting for transfers between devices, body(): arrived = lax.ppermute(sent, 'fsdp', ACROSS)  13.9 us
    all_to_all x1, waiting for transfers between devices, exchange(): lax.all_to_all(rows, axis, split_axis=0, concat_axis=0, tiled=True, axis_...  8.13 us
    all_to_all x1, starting transfers between devices, exchange(): lax.all_to_all(rows, axis, split_axis=0, concat_axis=0, tiled=True, axis_...  4.93 us
    pallas_call x1, Pallas kernels, normalise(): pl.pallas_call(norm_kernel, grid_spec=pltpu.PrefetchScalarGridSpec(num_sc...  4.51 us
  transfers between devices with their start and end apart: 13, of which 5 were waited for; matrix products, arithmetic and copies ran while one was open for 4% of the time, Pallas kernels for 9%

profile of v2, /device:TPU:20, one launch (start us, length us, event | category | flops | bytes accessed | tf_op | source)
XLA Modules:
  0.0 129.2 jit_solution(13035273141149781683)
XLA Ops:
  0.6 15.7 %collective-permute-start.9 = (bf16[512,512]{1,0:T(8,128)(2,1)}, bf16[512,512]{1,0:T(8,128)(2,1)S(1)}, u32[]{:S(2)}, u32[]{:S(2)}) collective-permute-start(bf16[512,512]{1,0:T(8,128)(2,1)} %bitcast.8), channel_id=1, source_target_pairs={{0,8},{1,9},{2,10},{3,11},{4,12},{5,13},{6,14},{7,15},{8,0},{9,1},... | collective-permute-start | bytes 1572872 | tf_op jit(solution)/shard_map/ppermute | solution.py:215
  17.0 51.3 %conditional.4 = (bf16[1024,1536]{1,0:T(8,128)(2,1)}, bf16[128,128]{1,0:T(8,128)(2,1)S(1)}, bf16[512,512]{1,0:T(8,128)(2,1)}) conditional(s32[]{:T(128)} %convert_element_type.40, () %tuple.45, (bf16[8192]{0:T(1024)(128)(2,1)}, bf16[128,8192]{1,0:T(8,128)(2,1)}, bf16[128,512]{1,0:T(8,128)(2,1)}, bf16[1,512,128]{2,1,0:T(8,128)(2,1)}, pred[]{:T(512)}) %tuple.46), branch_computations={%region_0.0_spmd, %region_1.4_spmd} | conditional | flops 262223 | bytes 11306137 | solution.py:158
  17.0 0.8 reshape.23.gain_ref
  17.9 4.5 %normalise.1 = bf16[8,128,1536]{2,1,0:T(8,128)(2,1)} custom-call(s32[1]{0:T(128)} %bitcast.1.half_ref, bf16[128,8192]{1,0:T(8,128)(2,1)} %get-tuple-element.78.acts_ref, bf16[1,8192]{1,0:T(2,128)(2,1)S(1)} %reshape.23.gain_ref, bf16[128,512]{1,0:T(8,128)(2,1)} %get-tuple-element.79.cot_ref), custom_call_target="tpu_custom_call" | custom-call | tf_op jit(solution)/shard_map/cond/branch_1_fun/normalise/pallas_call | solution.py:50
  22.4 4.9 %all-to-all-start.1 = ((bf16[8,128,1536]{2,1,0:T(8,128)(2,1)}), bf16[8,128,1536]{2,1,0:T(8,128)(2,1)}, u32[]{:S(2)}, u32[]{:S(2)}) async-start(bf16[8,128,1536]{2,1,0:T(8,128)(2,1)} %normalise.1), calls=%async_computation.1 | async-start | bytes 6291456 | tf_op jit(solution)/shard_map/cond/branch_1_fun/all_to_all | solution.py:162
  27.3 13.2 %conditional = (bf16[128,128]{1,0:T(8,128)(2,1)S(1)}) conditional(s32[]{:T(128)} %convert_element_type.33, () %tuple.30, bf16[512,128]{1,0:T(8,128)(2,1)S(1)} %bitcast.10), branch_computations={%region_2.2_spmd, %region_3.3_spmd} | conditional | flops 131133 | bytes 754462 | solution.py:158
  27.3 3.1 %collective-permute-start = (bf16[128,128]{1,0:T(8,128)(2,1)S(1)}, bf16[128,128]{1,0:T(8,128)(2,1)S(1)}, u32[]{:S(2)}, u32[]{:S(2)}) collective-permute-start(bf16[128,128]{1,0:T(8,128)(2,1)S(1)} %get-tuple-element.82), channel_id=1, source_target_pairs={{0,128},{16,144},{32,160},{48,176},{64,192},{80,208},{96,224},{112... | collective-permute-start | bytes 98312 | tf_op jit(solution)/shard_map/cond/branch_1_fun/cond/branch_1_fun/ppermute | solution.py:172
  30.4 2.7 %collective-permute-start.2 = (bf16[128,128]{1,0:T(8,128)(2,1)S(1)}, bf16[128,128]{1,0:T(8,128)(2,1)S(1)}, u32[]{:S(2)}, u32[]{:S(2)}) collective-permute-start(bf16[128,128]{1,0:T(8,128)(2,1)S(1)} %get-tuple-element.83), channel_id=1, source_target_pairs={{0,384},{16,400},{32,416},{48,432},{64,448},{80,464},{96,480},{112... | collective-permute-start | bytes 98312 | tf_op jit(solution)/shard_map/cond/branch_1_fun/cond/branch_1_fun/ppermute | solution.py:172
  33.2 3.6 %collective-permute-start.1 = (bf16[128,128]{1,0:T(8,128)(2,1)S(1)}, bf16[128,128]{1,0:T(8,128)(2,1)S(1)}, u32[]{:S(2)}, u32[]{:S(2)}) collective-permute-start(bf16[128,128]{1,0:T(8,128)(2,1)S(1)} %get-tuple-element.84), channel_id=1, source_target_pairs={{0,256},{16,272},{32,288},{48,304},{64,320},{80,336},{96,352},{112... | collective-permute-start | bytes 98312 | tf_op jit(solution)/shard_map/cond/branch_1_fun/cond/branch_1_fun/ppermute | solution.py:172
  36.8 3.6 %collective-permute-done.1 = bf16[128,128]{1,0:T(8,128)(2,1)S(1)} collective-permute-done((bf16[128,128]{1,0:T(8,128)(2,1)S(1)}, bf16[128,128]{1,0:T(8,128)(2,1)S(1)}, u32[]{:S(2)}, u32[]{:S(2)}) %collective-permute-start.1) | collective-permute-done | bytes 32800 | tf_op jit(solution)/shard_map/cond/branch_1_fun/cond/branch_1_fun/ppermute | solution.py:172
  40.5 5.2 %collective-permute-start.5 = (bf16[128,128]{1,0:T(8,128)(2,1)S(1)}, bf16[128,128]{1,0:T(8,128)(2,1)S(1)}, u32[]{:S(2)}, u32[]{:S(2)}) collective-permute-start(bf16[128,128]{1,0:T(8,128)(2,1)S(1)} %get-tuple-element.97), channel_id=1, source_target_pairs={{0,96},{16,112},{32,64},{48,80},{64,32},{80,48},{96,0},{112,16},{1... | collective-permute-start | bytes 98312 | tf_op jit(solution)/shard_map/cond/branch_1_fun/ppermute | solution.py:176
  45.7 3.7 %collective-permute-start.4 = (bf16[128,128]{1,0:T(8,128)(2,1)S(1)}, bf16[128,128]{1,0:T(8,128)(2,1)S(1)}, u32[]{:S(2)}, u32[]{:S(2)}) collective-permute-start(bf16[128,128]{1,0:T(8,128)(2,1)S(1)} %get-tuple-element.97), channel_id=1, source_target_pairs={{0,64},{16,80},{32,96},{48,112},{64,0},{80,16},{96,32},{112,48},{1... | collective-permute-start | bytes 98312 | tf_op jit(solution)/shard_map/cond/branch_1_fun/ppermute | solution.py:176
  49.4 5.2 %collective-permute-start.3 = (bf16[128,128]{1,0:T(8,128)(2,1)S(1)}, bf16[128,128]{1,0:T(8,128)(2,1)S(1)}, u32[]{:S(2)}, u32[]{:S(2)}) collective-permute-start(bf16[128,128]{1,0:T(8,128)(2,1)S(1)} %get-tuple-element.97), channel_id=1, source_target_pairs={{0,32},{16,48},{32,0},{48,16},{64,96},{80,112},{96,64},{112,80},{1... | collective-permute-start | bytes 98312 | tf_op jit(solution)/shard_map/cond/branch_1_fun/ppermute | solution.py:176
  54.6 8.1 %all-to-all-done.1 = bf16[8,128,1536]{2,1,0:T(8,128)(2,1)} async-done(((bf16[8,128,1536]{2,1,0:T(8,128)(2,1)}), bf16[8,128,1536]{2,1,0:T(8,128)(2,1)}, u32[]{:S(2)}, u32[]{:S(2)}) %all-to-all-start.1) | async-done | bytes 3145760 | tf_op jit(solution)/shard_map/cond/branch_1_fun/all_to_all | solution.py:162
  62.7 3.1 %far_gradient.1 = bf16[512,512]{1,0:T(8,128)(2,1)} custom-call(bf16[1024,1536]{1,0:T(8,128)(2,1)} %bitcast.2.normed_ref.cot_ref, bf16[1024,1536]{1,0:T(8,128)(2,1)} %bitcast.2.normed_ref.cot_ref), custom_call_target="tpu_custom_call" | custom-call | tf_op jit(solution)/shard_map/cond/branch_1_fun/far_gradient/pallas_call | solution.py:79
  65.8 2.5 %collective-permute-done.4 = bf16[128,128]{1,0:T(8,128)(2,1)S(1)} collective-permute-done((bf16[128,128]{1,0:T(8,128)(2,1)S(1)}, bf16[128,128]{1,0:T(8,128)(2,1)S(1)}, u32[]{:S(2)}, u32[]{:S(2)}) %collective-permute-start.4) | collective-permute-done | bytes 32800 | tf_op jit(solution)/shard_map/cond/branch_1_fun/ppermute | solution.py:176
  68.3 3.0 %collective-permute-start.10 = (bf16[512,512]{1,0:T(8,128)(2,1)}, bf16[512,512]{1,0:T(8,128)(2,1)S(1)}, u32[]{:S(2)}, u32[]{:S(2)}) collective-permute-start(bf16[512,512]{1,0:T(8,128)(2,1)} %get-tuple-element.64), channel_id=1, source_target_pairs={{0,8},{1,9},{2,10},{3,11},{4,12},{5,13},{6,14},{7,15},{8,0},{9,1},... | collective-permute-start | bytes 1572872 | tf_op jit(solution)/shard_map/ppermute | solution.py:232
  71.4 16.1 %conditional.5 = (f32[512,512]{1,0:T(8,128)S(1)}, bf16[512,128]{1,0:T(8,128)(2,1)}, bf16[1024,512]{1,0:T(8,128)(2,1)S(1)}) conditional(s32[]{:T(128)} %convert_element_type.40, () %tuple.44, (bf16[1024,1536]{1,0:T(8,128)(2,1)}, bf16[512,512]{1,0:T(8,128)(2,1)S(1)}, bf16[512,512]{1,0:T(8,128)(2,1)S(1)}, bf16[128,128]{1,0:T(8,128)(2,1)S(1)}) %tuple.60), branch_computations={%region_4.5_spmd, %region_5.6_spmd} | conditional | flops 62 | bytes 2884440 | solution.py:158
  71.4 2.4 %collective-permute-start.8 = (bf16[128,128]{1,0:T(8,128)(2,1)S(1)}, bf16[128,128]{1,0:T(8,128)(2,1)S(1)}, u32[]{:S(2)}, u32[]{:S(2)}) collective-permute-start(bf16[128,128]{1,0:T(8,128)(2,1)S(1)} %get-tuple-element.43), channel_id=1, source_target_pairs={{0,384},{16,400},{32,416},{48,432},{64,448},{80,464},{96,480},{112... | collective-permute-start | bytes 98312 | tf_op jit(solution)/shard_map/cond/branch_1_fun/ppermute | solution.py:172
  73.9 4.6 %collective-permute-start.7 = (bf16[128,128]{1,0:T(8,128)(2,1)S(1)}, bf16[128,128]{1,0:T(8,128)(2,1)S(1)}, u32[]{:S(2)}, u32[]{:S(2)}) collective-permute-start(bf16[128,128]{1,0:T(8,128)(2,1)S(1)} %get-tuple-element.43), channel_id=1, source_target_pairs={{0,256},{16,272},{32,288},{48,304},{64,320},{80,336},{96,352},{112... | collective-permute-start | bytes 98312 | tf_op jit(solution)/shard_map/cond/branch_1_fun/ppermute | solution.py:172
  78.5 2.0 %collective-permute-start.6 = (bf16[128,128]{1,0:T(8,128)(2,1)S(1)}, bf16[128,128]{1,0:T(8,128)(2,1)S(1)}, u32[]{:S(2)}, u32[]{:S(2)}) collective-permute-start(bf16[128,128]{1,0:T(8,128)(2,1)S(1)} %get-tuple-element.43), channel_id=1, source_target_pairs={{0,128},{16,144},{32,160},{48,176},{64,192},{80,208},{96,224},{112... | collective-permute-start | bytes 98312 | tf_op jit(solution)/shard_map/cond/branch_1_fun/ppermute | solution.py:172
  80.6 0.7 broadcast.36
  81.8 3.8 %near_work.1 = (bf16[1024,512]{1,0:T(8,128)(2,1)S(1)}, f32[512,512]{1,0:T(8,128)S(1)}) custom-call(bf16[1024,1536]{1,0:T(8,128)(2,1)} %get-tuple-element.39.mixed_ref, bf16[512,512]{1,0:T(8,128)(2,1)S(1)} %get-tuple-element.40.near_weight_ref, bf16[512,512]{1,0:T(8,128)(2,1)} %copy-done.3), custom_call_target="tpu_custom_call" | custom-call | tf_op jit(solution)/shard_map/cond/branch_1_fun/near_work/pallas_call | solution.py:104
  85.6 0.6 constant_dynamic-update-slice_fusion.2
  86.2 0.6 constant_dynamic-update-slice_fusion.1
  86.9 0.6 constant_dynamic-update-slice_fusion
  87.5 5.5 %collective-permute-start.11 = (bf16[512,128]{1,0:T(8,128)(2,1)}, bf16[512,128]{1,0:T(8,128)(2,1)S(1)}, u32[]{:S(2)}, u32[]{:S(2)}) collective-permute-start(bf16[512,128]{1,0:T(8,128)(2,1)} %get-tuple-element.65.ours_ref), channel_id=1, source_target_pairs={{0,16},{16,0},{32,48},{48,32},{64,80},{80,64},{96,112},{112,96},{1... | collective-permute-start | bytes 393224 | tf_op jit(solution)/shard_map/ppermute | solution.py:176
  93.0 19.0 %conditional.6 = (bf16[128,512]{1,0:T(8,128)(2,1)S(1)}) conditional(s32[]{:T(128)} %convert_element_type.40, () %tuple.43, bf16[1024,512]{1,0:T(8,128)(2,1)S(1)} %get-tuple-element.63), branch_computations={%region_6.7_spmd, %region_7.9_spmd} | conditional | flops 458752 | bytes 3276810 | solution.py:158
  93.1 17.6 %all_to_all.13 = bf16[8,128,512]{2,1,0:T(8,128)(2,1)} all-to-all(bf16[8,128,512]{2,1,0:T(8,128)(2,1)S(1)} %bitcast.7), channel_id=1, replica_groups={{0,1,2,3,4,5,6,7},{8,9,10,11,12,13,14,15},{16,17,18,19,20,21,22,23},{24..., dimensions={0} | all-to-all | bytes 2097152 | tf_op jit(solution)/shard_map/cond/branch_1_fun/all_to_all | solution.py:162
  110.7 1.4 %reduce_sum.11 = bf16[128,512]{1,0:T(8,128)(2,1)S(1)} reduce(bf16[8,128,512]{2,1,0:T(8,128)(2,1)} %all_to_all.13, bf16[]{:T(256)} %constant.122.clone), dimensions={0}, to_apply=%region_8.8 | reduce | flops 458752 | bytes 1179650 | tf_op jit(solution)/shard_map/cond/branch_1_fun/reduce_sum | solution.py:167
  112.1 13.9 %collective-permute-done.10.arrived_ref = bf16[512,512]{1,0:T(8,128)(2,1)S(1)} collective-permute-done((bf16[512,512]{1,0:T(8,128)(2,1)}, bf16[512,512]{1,0:T(8,128)(2,1)S(1)}, u32[]{:S(2)}, u32[]{:S(2)}) %collective-permute-start.10) | collective-permute-done | bytes 524320 | tf_op jit(solution)/shard_map/ppermute | solution.py:232
  126.0 3.2 %blend.1 = (bf16[512,512]{1,0:T(8,128)(2,1)}, f32[512,128]{1,0:T(8,128)}, f32[512,128]{1,0:T(8,128)}) custom-call(s32[1]{0:T(128)S(6)} %copy.36.start_ref, f32[512,512]{1,0:T(8,128)S(1)} %get-tuple-element.67.stepped_ref, bf16[512,512]{1,0:T(8,128)(2,1)S(1)} %collective-permute-done.10.arrived_ref, bf16[512,128]{1,0:T(8,128)(2,1)} %get-tuple-element.65.ours_ref, ...), custom_call_target="tpu_custom_call" | custom-call | tf_op jit(solution)/shard_map/blend/pallas_call | solution.py:137
  (25 shorter events, 0.8 us)
Async XLA Ops:
  0.6 70.7 %collective-permute-start.9 = (bf16[512,512]{1,0:T(8,128)(2,1)}, bf16[512,512]{1,0:T(8,128)(2,1)S(1)}, u32[]{:S(2)}, u32[]{:S(2)}) collective-permute-start(bf16[512,512]{1,0:T(8,128)(2,1)} %bitcast.8), channel_id=1, source_target_pairs={{0,8},{1,9},{2,10},{3,11},{4,12},{5,13},{6,14},{7,15},{8,0},{9,1},... | collective-permute-start | bytes 1572872 | tf_op jit(solution)/shard_map/ppermute | solution.py:215
  17.0 54.4 %copy-start.2 = (bf16[1,512,512]{2,1,0:T(8,128)(2,1)S(1)}, bf16[1,512,512]{2,1,0:T(8,128)(2,1)}, u32[]{:S(2)}) copy-start(bf16[1,512,512]{2,1,0:T(8,128)(2,1)} %param.18) | copy-start | bytes 1572868
  22.4 4.9 %copy-start.4 = (bf16[1,512,128]{2,1,0:T(8,128)(2,1)S(1)}, bf16[1,512,128]{2,1,0:T(8,128)(2,1)}, u32[]{:S(2)}) copy-start(bf16[1,512,128]{2,1,0:T(8,128)(2,1)} %get-tuple-element.81) | copy-start | bytes 393220 | tf_op jit(solution)/shard_map/cond
  22.4 40.3 %all-to-all-start.1 = ((bf16[8,128,1536]{2,1,0:T(8,128)(2,1)}), bf16[8,128,1536]{2,1,0:T(8,128)(2,1)}, u32[]{:S(2)}, u32[]{:S(2)}) async-start(bf16[8,128,1536]{2,1,0:T(8,128)(2,1)} %normalise.1), calls=%async_computation.1 | async-start | bytes 6291456 | tf_op jit(solution)/shard_map/cond/branch_1_fun/all_to_all | solution.py:162
  27.3 9.5 %collective-permute-start = (bf16[128,128]{1,0:T(8,128)(2,1)S(1)}, bf16[128,128]{1,0:T(8,128)(2,1)S(1)}, u32[]{:S(2)}, u32[]{:S(2)}) collective-permute-start(bf16[128,128]{1,0:T(8,128)(2,1)S(1)} %get-tuple-element.82), channel_id=1, source_target_pairs={{0,128},{16,144},{32,160},{48,176},{64,192},{80,208},{96,224},{112... | collective-permute-start | bytes 98312 | tf_op jit(solution)/shard_map/cond/branch_1_fun/cond/branch_1_fun/ppermute | solution.py:172
  30.4 6.4 %collective-permute-start.2 = (bf16[128,128]{1,0:T(8,128)(2,1)S(1)}, bf16[128,128]{1,0:T(8,128)(2,1)S(1)}, u32[]{:S(2)}, u32[]{:S(2)}) collective-permute-start(bf16[128,128]{1,0:T(8,128)(2,1)S(1)} %get-tuple-element.83), channel_id=1, source_target_pairs={{0,384},{16,400},{32,416},{48,432},{64,448},{80,464},{96,480},{112... | collective-permute-start | bytes 98312 | tf_op jit(solution)/shard_map/cond/branch_1_fun/cond/branch_1_fun/ppermute | solution.py:172
  33.2 7.3 %collective-permute-start.1 = (bf16[128,128]{1,0:T(8,128)(2,1)S(1)}, bf16[128,128]{1,0:T(8,128)(2,1)S(1)}, u32[]{:S(2)}, u32[]{:S(2)}) collective-permute-start(bf16[128,128]{1,0:T(8,128)(2,1)S(1)} %get-tuple-element.84), channel_id=1, source_target_pairs={{0,256},{16,272},{32,288},{48,304},{64,320},{80,336},{96,352},{112... | collective-permute-start | bytes 98312 | tf_op jit(solution)/shard_map/cond/branch_1_fun/cond/branch_1_fun/ppermute | solution.py:172
  40.5 25.3 %collective-permute-start.5 = (bf16[128,128]{1,0:T(8,128)(2,1)S(1)}, bf16[128,128]{1,0:T(8,128)(2,1)S(1)}, u32[]{:S(2)}, u32[]{:S(2)}) collective-permute-start(bf16[128,128]{1,0:T(8,128)(2,1)S(1)} %get-tuple-element.97), channel_id=1, source_target_pairs={{0,96},{16,112},{32,64},{48,80},{64,32},{80,48},{96,0},{112,16},{1... | collective-permute-start | bytes 98312 | tf_op jit(solution)/shard_map/cond/branch_1_fun/ppermute | solution.py:176
  45.7 22.6 %collective-permute-start.4 = (bf16[128,128]{1,0:T(8,128)(2,1)S(1)}, bf16[128,128]{1,0:T(8,128)(2,1)S(1)}, u32[]{:S(2)}, u32[]{:S(2)}) collective-permute-start(bf16[128,128]{1,0:T(8,128)(2,1)S(1)} %get-tuple-element.97), channel_id=1, source_target_pairs={{0,64},{16,80},{32,96},{48,112},{64,0},{80,16},{96,32},{112,48},{1... | collective-permute-start | bytes 98312 | tf_op jit(solution)/shard_map/cond/branch_1_fun/ppermute | solution.py:176
  49.4 18.9 %collective-permute-start.3 = (bf16[128,128]{1,0:T(8,128)(2,1)S(1)}, bf16[128,128]{1,0:T(8,128)(2,1)S(1)}, u32[]{:S(2)}, u32[]{:S(2)}) collective-permute-start(bf16[128,128]{1,0:T(8,128)(2,1)S(1)} %get-tuple-element.97), channel_id=1, source_target_pairs={{0,32},{16,48},{32,0},{48,16},{64,96},{80,112},{96,64},{112,80},{1... | collective-permute-start | bytes 98312 | tf_op jit(solution)/shard_map/cond/branch_1_fun/ppermute | solution.py:176
  68.3 57.6 %collective-permute-start.10 = (bf16[512,512]{1,0:T(8,128)(2,1)}, bf16[512,512]{1,0:T(8,128)(2,1)S(1)}, u32[]{:S(2)}, u32[]{:S(2)}) collective-permute-start(bf16[512,512]{1,0:T(8,128)(2,1)} %get-tuple-element.64), channel_id=1, source_target_pairs={{0,8},{1,9},{2,10},{3,11},{4,12},{5,13},{6,14},{7,15},{8,0},{9,1},... | collective-permute-start | bytes 1572872 | tf_op jit(solution)/shard_map/ppermute | solution.py:232
  71.4 10.4 %copy-start.3 = (bf16[512,512]{1,0:T(8,128)(2,1)}, bf16[512,512]{1,0:T(8,128)(2,1)S(1)}, u32[]{:S(2)}) copy-start(bf16[512,512]{1,0:T(8,128)(2,1)S(1)} %get-tuple-element.41.far_weight_ref) | copy-start | bytes 1572868 | tf_op jit(solution)/shard_map/cond
  71.4 15.4 %collective-permute-start.8 = (bf16[128,128]{1,0:T(8,128)(2,1)S(1)}, bf16[128,128]{1,0:T(8,128)(2,1)S(1)}, u32[]{:S(2)}, u32[]{:S(2)}) collective-permute-start(bf16[128,128]{1,0:T(8,128)(2,1)S(1)} %get-tuple-element.43), channel_id=1, source_target_pairs={{0,384},{16,400},{32,416},{48,432},{64,448},{80,464},{96,480},{112... | collective-permute-start | bytes 98312 | tf_op jit(solution)/shard_map/cond/branch_1_fun/ppermute | solution.py:172
  73.9 12.4 %collective-permute-start.7 = (bf16[128,128]{1,0:T(8,128)(2,1)S(1)}, bf16[128,128]{1,0:T(8,128)(2,1)S(1)}, u32[]{:S(2)}, u32[]{:S(2)}) collective-permute-start(bf16[128,128]{1,0:T(8,128)(2,1)S(1)} %get-tuple-element.43), channel_id=1, source_target_pairs={{0,256},{16,272},{32,288},{48,304},{64,320},{80,336},{96,352},{112... | collective-permute-start | bytes 98312 | tf_op jit(solution)/shard_map/cond/branch_1_fun/ppermute | solution.py:172
  78.5 7.1 %collective-permute-start.6 = (bf16[128,128]{1,0:T(8,128)(2,1)S(1)}, bf16[128,128]{1,0:T(8,128)(2,1)S(1)}, u32[]{:S(2)}, u32[]{:S(2)}) collective-permute-start(bf16[128,128]{1,0:T(8,128)(2,1)S(1)} %get-tuple-element.43), channel_id=1, source_target_pairs={{0,128},{16,144},{32,160},{48,176},{64,192},{80,208},{96,224},{112... | collective-permute-start | bytes 98312 | tf_op jit(solution)/shard_map/cond/branch_1_fun/ppermute | solution.py:172
  87.5 38.5 %copy-start = (f32[512,128]{1,0:T(8,128)S(1)}, f32[512,128]{1,0:T(8,128)}, u32[]{:S(2)}) copy-start(f32[512,128]{1,0:T(8,128)} %frag_ref.1) | copy-start | bytes 786436
  87.5 38.5 %copy-start.1 = (f32[512,128]{1,0:T(8,128)S(1)}, f32[512,128]{1,0:T(8,128)}, u32[]{:S(2)}) copy-start(f32[512,128]{1,0:T(8,128)} %mom_ref.1) | copy-start | bytes 786436
  87.5 38.5 %collective-permute-start.11 = (bf16[512,128]{1,0:T(8,128)(2,1)}, bf16[512,128]{1,0:T(8,128)(2,1)S(1)}, u32[]{:S(2)}, u32[]{:S(2)}) collective-permute-start(bf16[512,128]{1,0:T(8,128)(2,1)} %get-tuple-element.65.ours_ref), channel_id=1, source_target_pairs={{0,16},{16,0},{32,48},{48,32},{64,80},{80,64},{96,112},{112,96},{1... | collective-permute-start | bytes 393224 | tf_op jit(solution)/shard_map/ppermute | solution.py:176
  112.1 17.1 %copy-start.5 = (bf16[128,512]{1,0:T(8,128)(2,1)}, bf16[128,512]{1,0:T(8,128)(2,1)S(1)}, u32[]{:S(2)}) copy-start(bf16[128,512]{1,0:T(8,128)(2,1)S(1)} %get-tuple-element.98) | copy-start | bytes 393220

commit v3 on v2

--- a/solution.py
+++ b/solution.py
@@ -12,6 +12,9 @@
 BLOCK = 512
 KVW = 512
 HD = 128
+JOIN_COST = pl.CostEstimate(flops=11500000000, bytes_accessed=10**6, transcendentals=0)
+HOLD_COST = pl.CostEstimate(flops=26450000000, bytes_accessed=10**6, transcendentals=0)
+SHORT = pl.CostEstimate(flops=10**6, bytes_accessed=10**4, transcendentals=0)
 REPLICAS = 32
 INV_ROOT = D ** (-0.5)
 
@@ -61,6 +64,7 @@
         ),
         out_shape=jax.ShapeDtypeStruct((HALF, ROWS_IN, WIDE), jnp.bfloat16),
         compiler_params=pltpu.CompilerParams(vmem_limit_bytes=32 * 1024 * 1024),
+        cost_estimate=SHORT,
         name="normalise",
     )(half, acts, gain, cot)
 
@@ -86,6 +90,7 @@
         out_specs=pl.BlockSpec((step, KVW), lambda i: (i, 0)),
         out_shape=jax.ShapeDtypeStruct((BLOCK, KVW), jnp.bfloat16),
         compiler_params=pltpu.CompilerParams(vmem_limit_bytes=32 * 1024 * 1024),
+        cost_estimate=SHORT,
         name="far_gradient",
     )(mixed, mixed)
 
@@ -190,14 +195,41 @@
     return total.astype(jnp.bfloat16)
 
 
-def spread_x(total):
-    blocks = [total] + [turned(total, by) for by in range(1, 4)]
-    x = own_x()
-    out = jnp.zeros((4 * total.shape[0], total.shape[1]), total.dtype)
-    for by in range(4):
-        at = lax.rem(x + 4 - by, 4) * total.shape[0]
-        out = lax.dynamic_update_slice_in_dim(out, blocks[by], at, 0)
-    return out
+def hold_kernel(in_ref, out_ref):
+    out_ref[...] = in_ref[...]
+
+
+def hold(rows):
+    return pl.pallas_call(
+        hold_kernel,
+        out_shape=jax.ShapeDtypeStruct(rows.shape, rows.dtype),
+        in_specs=[pl.BlockSpec(memory_space=pltpu.VMEM)],
+        out_specs=pl.BlockSpec(memory_space=pltpu.VMEM),
+        compiler_params=pltpu.CompilerParams(vmem_limit_bytes=16 * 1024 * 1024),
+        cost_estimate=HOLD_COST,
+        name="hold",
+    )(rows)
+
+
+def join_kernel(x_ref, a_ref, b_ref, c_ref, d_ref, out_ref):
+    x = x_ref[0]
+    part = a_ref.shape[0]
+    for by, ref in enumerate((a_ref, b_ref, c_ref, d_ref)):
+        at = pl.multiple_of(lax.rem(x + 4 - by, 4) * part, part)
+        out_ref[pl.ds(at, part), :] = ref[...]
+
+
+def join(blocks):
+    part, width = blocks[0].shape
+    return pl.pallas_call(
+        join_kernel,
+        out_shape=jax.ShapeDtypeStruct((4 * part, width), jnp.bfloat16),
+        in_specs=[pl.BlockSpec(memory_space=pltpu.SMEM)] + [pl.BlockSpec(memory_space=pltpu.VMEM)] * 4,
+        out_specs=pl.BlockSpec(memory_space=pltpu.VMEM),
+        compiler_params=pltpu.CompilerParams(vmem_limit_bytes=16 * 1024 * 1024),
+        cost_estimate=JOIN_COST,
+        name="join",
+    )(own_x().astype(jnp.int32).reshape(1), *blocks)
 
 
 def body(
@@ -214,28 +246,29 @@
     go = fragment_index[0] >= 0
     far_weight = lax.ppermute(weight, "fsdp", ACROSS)
 
-    def first(acts, gain, cot, delta):
-        half = (lax.axis_index("fsdp") // HALF).astype(jnp.int32).reshape(1)
-        mixed = normalise(half, acts, gain.reshape(1, D), cot)
-        delta, mixed = lax.optimization_barrier((delta, mixed))
-        mixed = exchange(mixed.reshape(HALF * ROWS_IN, WIDE), "fsdp", HALVES)
-        own = staged(go, reduce_x, delta)
-        arrivals = [paired(own, bits) for bits in (2, 4, 6)]
-        sent = far_gradient(mixed)
-        arrivals, own, sent = lax.optimization_barrier((arrivals, own, sent))
-        total = own.astype(jnp.float32)
-        for arrived in arrivals:
-            total += arrived.astype(jnp.float32)
-        return mixed, total.astype(jnp.bfloat16), sent
-
-    mixed, some, sent = staged(go, first, acts, norm_gain, key_cotangent, pending_delta[0])
+    half = (lax.axis_index("fsdp") // HALF).astype(jnp.int32).reshape(1)
+    mixed = normalise(half, acts, norm_gain.reshape(1, D), key_cotangent)
+    delta, mixed = lax.optimization_barrier((pending_delta[0], mixed))
+    mixed = exchange(mixed.reshape(HALF * ROWS_IN, WIDE), "fsdp", HALVES)
+    own = staged(go, reduce_x, delta)
+    arrivals = [paired(own, bits) for bits in (2, 4, 6)]
+    far_weight = hold(far_weight)
+    mixed, far_weight = lax.optimization_barrier((mixed, far_weight))
+    sent = far_gradient(mixed)
     arrived = lax.ppermute(sent, "fsdp", ACROSS)
 
-    def second(mixed, some, weight, far_weight):
+    def second(mixed, own, arrivals, weight, far_weight):
+        some = own.astype(jnp.float32)
+        for part in arrivals:
+            some += part.astype(jnp.float32)
+        some = some.astype(jnp.bfloat16)
+        blocks = [some] + [turned(some, by) for by in range(1, 4)]
         keys, stepped = near_work(mixed, weight, far_weight)
-        return keys, stepped, spread_x(some)
-
-    keys, stepped, ours = staged(go, second, mixed, some, weight, far_weight)
+        return keys, stepped, blocks
+
+    keys, stepped, blocks = staged(go, second, mixed, own, arrivals, weight, far_weight)
+    ours = join(blocks)
+    keys, ours = lax.optimization_barrier((keys, ours))
     theirs = paired(ours, 1)
 
     def third(keys):

time: 130 us -> 128 us (0.985)
  the two profiles are of different devices: /device:TPU:20 before, /device:TPU:34 now
where the time goes in v3:
time: 128 us; the launch traced here: 127 us
  starting transfers between devices  65.8 us (51%)
  waiting for transfers between devices  22.1 us (17%)
  blocking collectives  20.5 us (16%)
  Pallas kernels  11.6 us (9%)
  local copies, waits for them, and re-layouts  3.27 us (3%)
  other arithmetic  2.03 us (2%)
  between operations  1.49 us (1%)
    ppermute x6, starting transfers between devices, turned(): return lax.ppermute(rows, 'replica', ring)  21.3 us
    all_to_all x1, blocking collectives, exchange(): lax.all_to_all(rows, axis, split_axis=0, concat_axis=0, tiled=True, axis_...  20.5 us
    ppermute x4, starting transfers between devices, paired(): lax.ppermute(rows, 'replica', [(r, r ^ bits) for r in range(REPLICAS)])  16.1 us
    ppermute x1, starting transfers between devices, body(): far_weight = lax.ppermute(weight, 'fsdp', ACROSS)  14.8 us
    ppermute x1, waiting for transfers between devices, body(): far_weight = lax.ppermute(weight, 'fsdp', ACROSS)  9.3 us
    ppermute x1, starting transfers between devices, body(): arrived = lax.ppermute(sent, 'fsdp', ACROSS)  9.03 us
    ppermute x4, waiting for transfers between devices, paired(): lax.ppermute(rows, 'replica', [(r, r ^ bits) for r in range(REPLICAS)])  7.95 us
    all_to_all x1, starting transfers between devices, exchange(): lax.all_to_all(rows, axis, split_axis=0, concat_axis=0, tiled=True, axis_...  4.6 us
  transfers between devices with their start and end apart: 13, of which 6 were waited for; matrix products, arithmetic and copies ran while one was open for 2% of the time, Pallas kernels for 8%

profile of v3, /device:TPU:34, one launch (start us, length us, event | category | flops | bytes accessed | tf_op | source)
XLA Modules:
  0.0 127.0 jit_solution(12949775129637167069)
XLA Ops:
  0.6 14.8 %collective-permute-start.6 = (bf16[512,512]{1,0:T(8,128)(2,1)}, bf16[512,512]{1,0:T(8,128)(2,1)S(1)}, u32[]{:S(2)}, u32[]{:S(2)}) collective-permute-start(bf16[512,512]{1,0:T(8,128)(2,1)} %bitcast.9), channel_id=1, source_target_pairs={{0,8},{1,9},{2,10},{3,11},{4,12},{5,13},{6,14},{7,15},{8,0},{9,1},... | collective-permute-start | bytes 1572872 | tf_op jit(solution)/shard_map/ppermute | solution.py:247
  15.5 0.7 reshape.30.gain_ref
  16.2 1.6 %copy-done = bf16[128,8192]{1,0:T(8,128)(2,1)S(1)} copy-done((bf16[128,8192]{1,0:T(8,128)(2,1)S(1)}, bf16[128,8192]{1,0:T(8,128)(2,1)}, u32[]{:S(2)}) %copy-start) | copy-done | bytes 2097176
  17.8 0.9 copy-done.3
  18.7 2.7 %normalise.1 = bf16[8,128,1536]{2,1,0:T(8,128)(2,1)} custom-call(s32[1]{0:T(128)} %bitcast.3.half_ref, bf16[128,8192]{1,0:T(8,128)(2,1)S(1)} %copy-done, bf16[1,8192]{1,0:T(2,128)(2,1)S(1)} %reshape.30.gain_ref, bf16[128,512]{1,0:T(8,128)(2,1)S(1)} %copy-done.3), custom_call_target="tpu_custom_call" | custom-call | flops 1000000 | bytes 10000 | tf_op jit(solution)/shard_map/normalise/pallas_call | solution.py:53
  21.5 4.6 %all-to-all-start.1 = ((bf16[8,128,1536]{2,1,0:T(8,128)(2,1)}), bf16[8,128,1536]{2,1,0:T(8,128)(2,1)}, u32[]{:S(2)}, u32[]{:S(2)}) async-start(bf16[8,128,1536]{2,1,0:T(8,128)(2,1)} %normalise.1), calls=%async_computation.1 | async-start | bytes 6291456 | tf_op jit(solution)/shard_map/all_to_all | solution.py:167
  26.7 12.4 %conditional.3 = (bf16[128,128]{1,0:T(8,128)(2,1)S(1)}) conditional(s32[]{:T(128)} %bitcast.1, () %tuple.36, bf16[512,128]{1,0:T(8,128)(2,1)S(1)} %bitcast.11), branch_computations={%region_0.1_spmd, %region_1.2_spmd} | conditional | flops 131133 | bytes 754462 | solution.py:163
  26.8 3.4 %collective-permute-start = (bf16[128,128]{1,0:T(8,128)(2,1)S(1)}, bf16[128,128]{1,0:T(8,128)(2,1)S(1)}, u32[]{:S(2)}, u32[]{:S(2)}) collective-permute-start(bf16[128,128]{1,0:T(8,128)(2,1)S(1)} %get-tuple-element.71), channel_id=1, source_target_pairs={{0,128},{16,144},{32,160},{48,176},{64,192},{80,208},{96,224},{112... | collective-permute-start | bytes 98312 | tf_op jit(solution)/shard_map/cond/branch_1_fun/ppermute | solution.py:177
  30.2 3.0 %collective-permute-start.1 = (bf16[128,128]{1,0:T(8,128)(2,1)S(1)}, bf16[128,128]{1,0:T(8,128)(2,1)S(1)}, u32[]{:S(2)}, u32[]{:S(2)}) collective-permute-start(bf16[128,128]{1,0:T(8,128)(2,1)S(1)} %get-tuple-element.73), channel_id=1, source_target_pairs={{0,256},{16,272},{32,288},{48,304},{64,320},{80,336},{96,352},{112... | collective-permute-start | bytes 98312 | tf_op jit(solution)/shard_map/cond/branch_1_fun/ppermute | solution.py:177
  33.3 4.1 %collective-permute-start.2 = (bf16[128,128]{1,0:T(8,128)(2,1)S(1)}, bf16[128,128]{1,0:T(8,128)(2,1)S(1)}, u32[]{:S(2)}, u32[]{:S(2)}) collective-permute-start(bf16[128,128]{1,0:T(8,128)(2,1)S(1)} %get-tuple-element.72), channel_id=1, source_target_pairs={{0,384},{16,400},{32,416},{48,432},{64,448},{80,464},{96,480},{112... | collective-permute-start | bytes 98312 | tf_op jit(solution)/shard_map/cond/branch_1_fun/ppermute | solution.py:177
  37.6 1.5 %collective-permute-done.2 = bf16[128,128]{1,0:T(8,128)(2,1)S(1)} collective-permute-done((bf16[128,128]{1,0:T(8,128)(2,1)S(1)}, bf16[128,128]{1,0:T(8,128)(2,1)S(1)}, u32[]{:S(2)}, u32[]{:S(2)}) %collective-permute-start.2) | collective-permute-done | bytes 32800 | tf_op jit(solution)/shard_map/cond/branch_1_fun/ppermute | solution.py:177
  39.1 3.4 %collective-permute-start.7 = (bf16[128,128]{1,0:T(8,128)(2,1)S(1)}, bf16[128,128]{1,0:T(8,128)(2,1)S(1)}, u32[]{:S(2)}, u32[]{:S(2)}) collective-permute-start(bf16[128,128]{1,0:T(8,128)(2,1)S(1)} %get-tuple-element.86), channel_id=1, source_target_pairs={{0,32},{16,48},{32,0},{48,16},{64,96},{80,112},{96,64},{112,80},{1... | collective-permute-start | bytes 98312 | tf_op jit(solution)/shard_map/ppermute | solution.py:181
  42.5 4.3 %collective-permute-start.8 = (bf16[128,128]{1,0:T(8,128)(2,1)S(1)}, bf16[128,128]{1,0:T(8,128)(2,1)S(1)}, u32[]{:S(2)}, u32[]{:S(2)}) collective-permute-start(bf16[128,128]{1,0:T(8,128)(2,1)S(1)} %get-tuple-element.86), channel_id=1, source_target_pairs={{0,64},{16,80},{32,96},{48,112},{64,0},{80,16},{96,32},{112,48},{1... | collective-permute-start | bytes 98312 | tf_op jit(solution)/shard_map/ppermute | solution.py:181
  46.8 6.3 %collective-permute-start.9 = (bf16[128,128]{1,0:T(8,128)(2,1)S(1)}, bf16[128,128]{1,0:T(8,128)(2,1)S(1)}, u32[]{:S(2)}, u32[]{:S(2)}) collective-permute-start(bf16[128,128]{1,0:T(8,128)(2,1)S(1)} %get-tuple-element.86), channel_id=1, source_target_pairs={{0,96},{16,112},{32,64},{48,80},{64,32},{80,48},{96,0},{112,16},{1... | collective-permute-start | bytes 98312 | tf_op jit(solution)/shard_map/ppermute | solution.py:181
  53.2 9.3 %collective-permute-done.6.in_ref = bf16[512,512]{1,0:T(8,128)(2,1)S(1)} collective-permute-done((bf16[512,512]{1,0:T(8,128)(2,1)}, bf16[512,512]{1,0:T(8,128)(2,1)S(1)}, u32[]{:S(2)}, u32[]{:S(2)}) %collective-permute-start.6) | collective-permute-done | bytes 524320 | tf_op jit(solution)/shard_map/ppermute | solution.py:247
  62.5 2.1 %all-to-all-done.1 = bf16[8,128,1536]{2,1,0:T(8,128)(2,1)} async-done(((bf16[8,128,1536]{2,1,0:T(8,128)(2,1)}), bf16[8,128,1536]{2,1,0:T(8,128)(2,1)}, u32[]{:S(2)}, u32[]{:S(2)}) %all-to-all-start.1) | async-done | bytes 3145760 | tf_op jit(solution)/shard_map/all_to_all | solution.py:167
  64.6 2.4 %far_gradient.1 = bf16[512,512]{1,0:T(8,128)(2,1)S(1)} custom-call(bf16[1024,1536]{1,0:T(8,128)(2,1)} %bitcast.4.normed_ref.cot_ref, bf16[1024,1536]{1,0:T(8,128)(2,1)} %bitcast.4.normed_ref.cot_ref), custom_call_target="tpu_custom_call" | custom-call | flops 1000000 | bytes 10000 | tf_op jit(solution)/shard_map/far_gradient/pallas_call | solution.py:83
  67.0 9.0 %collective-permute-start.10 = (bf16[512,512]{1,0:T(8,128)(2,1)S(1)}, bf16[512,512]{1,0:T(8,128)(2,1)S(1)}, u32[]{:S(2)}, u32[]{:S(2)}) collective-permute-start(bf16[512,512]{1,0:T(8,128)(2,1)S(1)} %far_gradient.1), channel_id=1, source_target_pairs={{0,8},{1,9},{2,10},{3,11},{4,12},{5,13},{6,14},{7,15},{8,0},{9,1},... | collective-permute-start | bytes 1572872 | tf_op jit(solution)/shard_map/ppermute | solution.py:258
  76.1 15.2 %conditional.4 = (bf16[1024,512]{1,0:T(8,128)(2,1)S(1)}, f32[512,512]{1,0:T(8,128)S(1)}, bf16[128,128]{1,0:T(8,128)(2,1)}, bf16[128,128]{1,0:T(8,128)(2,1)}, bf1...) conditional(s32[]{:T(128)} %bitcast.1, () %tuple.33, (bf16[1024,1536]{1,0:T(8,128)(2,1)}, ...), branch_computations={%region_2.3_spmd, %region_3.4_spmd} | conditional | flops 131072 | bytes 2228286 | solution.py:163
  76.1 0.6 add_convert_fusion.1
  76.8 3.5 %collective-permute-start.3 = (bf16[128,128]{1,0:T(8,128)(2,1)}, bf16[128,128]{1,0:T(8,128)(2,1)}, u32[]{:S(2)}, u32[]{:S(2)}) collective-permute-start(bf16[128,128]{1,0:T(8,128)(2,1)} %add_convert_fusion.1), channel_id=1, source_target_pairs={{0,128},{16,144},{32,160},{48,176},{64,192},{80,208},{96,224},{112... | collective-permute-start | bytes 98312 | tf_op jit(solution)/shard_map/cond/branch_1_fun/ppermute | solution.py:177
  80.3 3.3 %collective-permute-start.4 = (bf16[128,128]{1,0:T(8,128)(2,1)}, bf16[128,128]{1,0:T(8,128)(2,1)}, u32[]{:S(2)}, u32[]{:S(2)}) collective-permute-start(bf16[128,128]{1,0:T(8,128)(2,1)} %add_convert_fusion.1), channel_id=1, source_target_pairs={{0,256},{16,272},{32,288},{48,304},{64,320},{80,336},{96,352},{112... | collective-permute-start | bytes 98312 | tf_op jit(solution)/shard_map/cond/branch_1_fun/ppermute | solution.py:177
  83.6 4.0 %collective-permute-start.5 = (bf16[128,128]{1,0:T(8,128)(2,1)}, bf16[128,128]{1,0:T(8,128)(2,1)}, u32[]{:S(2)}, u32[]{:S(2)}) collective-permute-start(bf16[128,128]{1,0:T(8,128)(2,1)} %add_convert_fusion.1), channel_id=1, source_target_pairs={{0,384},{16,400},{32,416},{48,432},{64,448},{80,464},{96,480},{112... | collective-permute-start | bytes 98312 | tf_op jit(solution)/shard_map/cond/branch_1_fun/ppermute | solution.py:177
  87.6 3.7 %near_work.1 = (bf16[1024,512]{1,0:T(8,128)(2,1)S(1)}, f32[512,512]{1,0:T(8,128)S(1)}) custom-call(bf16[1024,1536]{1,0:T(8,128)(2,1)} %get-tuple-element.22.mixed_ref, bf16[512,512]{1,0:T(8,128)(2,1)S(1)} %get-tuple-element.23.near_weight_ref, bf16[512,512]{1,0:T(8,128)(2,1)S(1)} %get-tuple-element.24.far_weight_ref), custom_call_target="tpu_custom_call" | custom-call | tf_op jit(solution)/shard_map/cond/branch_1_fun/near_work/pallas_call | solution.py:109
  91.3 0.8 join.1.ours_ref
  92.2 2.1 %collective-permute-start.11 = (bf16[512,128]{1,0:T(8,128)(2,1)S(1)}, bf16[512,128]{1,0:T(8,128)(2,1)S(1)}, u32[]{:S(2)}, u32[]{:S(2)}) collective-permute-start(bf16[512,128]{1,0:T(8,128)(2,1)S(1)} %join.1.ours_ref), channel_id=1, source_target_pairs={{0,16},{16,0},{32,48},{48,32},{64,80},{80,64},{96,112},{112,96},{1... | collective-permute-start | bytes 393224 | tf_op jit(solution)/shard_map/ppermute | solution.py:181
  94.3 21.9 %conditional.5 = (bf16[128,512]{1,0:T(8,128)(2,1)S(1)}) conditional(s32[]{:T(128)} %bitcast.1, () %tuple.32, bf16[1024,512]{1,0:T(8,128)(2,1)S(1)} %get-tuple-element.62), branch_computations={%region_4.5_spmd, %region_5.7_spmd} | conditional | flops 458752 | bytes 3276810 | solution.py:163
  94.3 20.5 %all_to_all.16 = bf16[8,128,512]{2,1,0:T(8,128)(2,1)} all-to-all(bf16[8,128,512]{2,1,0:T(8,128)(2,1)S(1)} %bitcast.8), channel_id=1, replica_groups={{0,1,2,3,4,5,6,7},{8,9,10,11,12,13,14,15},{16,17,18,19,20,21,22,23},{24..., dimensions={0} | all-to-all | bytes 2097152 | tf_op jit(solution)/shard_map/cond/branch_1_fun/all_to_all | solution.py:167
  114.7 1.4 %reduce_sum.11 = bf16[128,512]{1,0:T(8,128)(2,1)S(1)} reduce(bf16[8,128,512]{2,1,0:T(8,128)(2,1)} %all_to_all.16, bf16[]{:T(256)} %constant.75.clone), dimensions={0}, to_apply=%region_6.6 | reduce | flops 458752 | bytes 1179650 | tf_op jit(solution)/shard_map/cond/branch_1_fun/reduce_sum | solution.py:172
  116.1 7.9 %collective-permute-done.11.theirs_ref = bf16[512,128]{1,0:T(8,128)(2,1)S(1)} collective-permute-done((bf16[512,128]{1,0:T(8,128)(2,1)S(1)}, bf16[512,128]{1,0:T(8,128)(2,1)S(1)}, u32[]{:S(2)}, u32[]{:S(2)}) %collective-permute-start.11) | collective-permute-done | bytes 131104 | tf_op jit(solution)/shard_map/ppermute | solution.py:181
  124.1 1.0 collective-permute-done.10.arrived_ref
  125.1 1.9 %blend.1 = (bf16[512,512]{1,0:T(8,128)(2,1)}, f32[512,128]{1,0:T(8,128)}, f32[512,128]{1,0:T(8,128)}) custom-call(s32[1]{0:T(128)S(6)} %copy.28.start_ref, f32[512,512]{1,0:T(8,128)S(1)} %get-tuple-element.65.stepped_ref, bf16[512,512]{1,0:T(8,128)(2,1)S(1)} %collective-permute-done.10.arrived_ref, bf16[512,128]{1,0:T(8,128)(2,1)S(1)} %join.1.ours_ref, ...), custom_call_target="tpu_custom_call" | custom-call | tf_op jit(solution)/shard_map/blend/pallas_call | solution.py:142
  (23 shorter events, 0.3 us)
Async XLA Ops:
  0.6 61.8 %collective-permute-start.6 = (bf16[512,512]{1,0:T(8,128)(2,1)}, bf16[512,512]{1,0:T(8,128)(2,1)S(1)}, u32[]{:S(2)}, u32[]{:S(2)}) collective-permute-start(bf16[512,512]{1,0:T(8,128)(2,1)} %bitcast.9), channel_id=1, source_target_pairs={{0,8},{1,9},{2,10},{3,11},{4,12},{5,13},{6,14},{7,15},{8,0},{9,1},... | collective-permute-start | bytes 1572872 | tf_op jit(solution)/shard_map/ppermute | solution.py:247
  16.2 1.6 %copy-start = (bf16[128,8192]{1,0:T(8,128)(2,1)S(1)}, bf16[128,8192]{1,0:T(8,128)(2,1)}, u32[]{:S(2)}) copy-start(bf16[128,8192]{1,0:T(8,128)(2,1)} %acts_ref.1) | copy-start | bytes 6291460
  17.8 0.9 copy-start.3
  21.5 5.3 %copy-start.5 = (bf16[1,512,128]{2,1,0:T(8,128)(2,1)S(1)}, bf16[1,512,128]{2,1,0:T(8,128)(2,1)}, u32[]{:S(2)}) copy-start(bf16[1,512,128]{2,1,0:T(8,128)(2,1)} %param.18) | copy-start | bytes 393220
  21.5 43.1 %all-to-all-start.1 = ((bf16[8,128,1536]{2,1,0:T(8,128)(2,1)}), bf16[8,128,1536]{2,1,0:T(8,128)(2,1)}, u32[]{:S(2)}, u32[]{:S(2)}) async-start(bf16[8,128,1536]{2,1,0:T(8,128)(2,1)} %normalise.1), calls=%async_computation.1 | async-start | bytes 6291456 | tf_op jit(solution)/shard_map/all_to_all | solution.py:167
  26.8 10.5 %collective-permute-start = (bf16[128,128]{1,0:T(8,128)(2,1)S(1)}, bf16[128,128]{1,0:T(8,128)(2,1)S(1)}, u32[]{:S(2)}, u32[]{:S(2)}) collective-permute-start(bf16[128,128]{1,0:T(8,128)(2,1)S(1)} %get-tuple-element.71), channel_id=1, source_target_pairs={{0,128},{16,144},{32,160},{48,176},{64,192},{80,208},{96,224},{112... | collective-permute-start | bytes 98312 | tf_op jit(solution)/shard_map/cond/branch_1_fun/ppermute | solution.py:177
  30.2 7.3 %collective-permute-start.1 = (bf16[128,128]{1,0:T(8,128)(2,1)S(1)}, bf16[128,128]{1,0:T(8,128)(2,1)S(1)}, u32[]{:S(2)}, u32[]{:S(2)}) collective-permute-start(bf16[128,128]{1,0:T(8,128)(2,1)S(1)} %get-tuple-element.73), channel_id=1, source_target_pairs={{0,256},{16,272},{32,288},{48,304},{64,320},{80,336},{96,352},{112... | collective-permute-start | bytes 98312 | tf_op jit(solution)/shard_map/cond/branch_1_fun/ppermute | solution.py:177
  33.3 5.8 %collective-permute-start.2 = (bf16[128,128]{1,0:T(8,128)(2,1)S(1)}, bf16[128,128]{1,0:T(8,128)(2,1)S(1)}, u32[]{:S(2)}, u32[]{:S(2)}) collective-permute-start(bf16[128,128]{1,0:T(8,128)(2,1)S(1)} %get-tuple-element.72), channel_id=1, source_target_pairs={{0,384},{16,400},{32,416},{48,432},{64,448},{80,464},{96,480},{112... | collective-permute-start | bytes 98312 | tf_op jit(solution)/shard_map/cond/branch_1_fun/ppermute | solution.py:177
  39.1 37.0 %collective-permute-start.7 = (bf16[128,128]{1,0:T(8,128)(2,1)S(1)}, bf16[128,128]{1,0:T(8,128)(2,1)S(1)}, u32[]{:S(2)}, u32[]{:S(2)}) collective-permute-start(bf16[128,128]{1,0:T(8,128)(2,1)S(1)} %get-tuple-element.86), channel_id=1, source_target_pairs={{0,32},{16,48},{32,0},{48,16},{64,96},{80,112},{96,64},{112,80},{1... | collective-permute-start | bytes 98312 | tf_op jit(solution)/shard_map/ppermute | solution.py:181
  42.5 33.6 %collective-permute-start.8 = (bf16[128,128]{1,0:T(8,128)(2,1)S(1)}, bf16[128,128]{1,0:T(8,128)(2,1)S(1)}, u32[]{:S(2)}, u32[]{:S(2)}) collective-permute-start(bf16[128,128]{1,0:T(8,128)(2,1)S(1)} %get-tuple-element.86), channel_id=1, source_target_pairs={{0,64},{16,80},{32,96},{48,112},{64,0},{80,16},{96,32},{112,48},{1... | collective-permute-start | bytes 98312 | tf_op jit(solution)/shard_map/ppermute | solution.py:181
  46.8 29.3 %collective-permute-start.9 = (bf16[128,128]{1,0:T(8,128)(2,1)S(1)}, bf16[128,128]{1,0:T(8,128)(2,1)S(1)}, u32[]{:S(2)}, u32[]{:S(2)}) collective-permute-start(bf16[128,128]{1,0:T(8,128)(2,1)S(1)} %get-tuple-element.86), channel_id=1, source_target_pairs={{0,96},{16,112},{32,64},{48,80},{64,32},{80,48},{96,0},{112,16},{1... | collective-permute-start | bytes 98312 | tf_op jit(solution)/shard_map/ppermute | solution.py:181
  64.6 11.5 %copy-start.4 = (bf16[1,512,512]{2,1,0:T(8,128)(2,1)S(1)}, bf16[1,512,512]{2,1,0:T(8,128)(2,1)}, u32[]{:S(2)}) copy-start(bf16[1,512,512]{2,1,0:T(8,128)(2,1)} %param.16) | copy-start | bytes 1572868
  67.0 58.0 %collective-permute-start.10 = (bf16[512,512]{1,0:T(8,128)(2,1)S(1)}, bf16[512,512]{1,0:T(8,128)(2,1)S(1)}, u32[]{:S(2)}, u32[]{:S(2)}) collective-permute-start(bf16[512,512]{1,0:T(8,128)(2,1)S(1)} %far_gradient.1), channel_id=1, source_target_pairs={{0,8},{1,9},{2,10},{3,11},{4,12},{5,13},{6,14},{7,15},{8,0},{9,1},... | collective-permute-start | bytes 1572872 | tf_op jit(solution)/shard_map/ppermute | solution.py:258
  76.8 14.5 %collective-permute-start.3 = (bf16[128,128]{1,0:T(8,128)(2,1)}, bf16[128,128]{1,0:T(8,128)(2,1)}, u32[]{:S(2)}, u32[]{:S(2)}) collective-permute-start(bf16[128,128]{1,0:T(8,128)(2,1)} %add_convert_fusion.1), channel_id=1, source_target_pairs={{0,128},{16,144},{32,160},{48,176},{64,192},{80,208},{96,224},{112... | collective-permute-start | bytes 98312 | tf_op jit(solution)/shard_map/cond/branch_1_fun/ppermute | solution.py:177
  80.3 11.0 %collective-permute-start.4 = (bf16[128,128]{1,0:T(8,128)(2,1)}, bf16[128,128]{1,0:T(8,128)(2,1)}, u32[]{:S(2)}, u32[]{:S(2)}) collective-permute-start(bf16[128,128]{1,0:T(8,128)(2,1)} %add_convert_fusion.1), channel_id=1, source_target_pairs={{0,256},{16,272},{32,288},{48,304},{64,320},{80,336},{96,352},{112... | collective-permute-start | bytes 98312 | tf_op jit(solution)/shard_map/cond/branch_1_fun/ppermute | solution.py:177
  83.6 7.8 %collective-permute-start.5 = (bf16[128,128]{1,0:T(8,128)(2,1)}, bf16[128,128]{1,0:T(8,128)(2,1)}, u32[]{:S(2)}, u32[]{:S(2)}) collective-permute-start(bf16[128,128]{1,0:T(8,128)(2,1)} %add_convert_fusion.1), channel_id=1, source_target_pairs={{0,384},{16,400},{32,416},{48,432},{64,448},{80,464},{96,480},{112... | collective-permute-start | bytes 98312 | tf_op jit(solution)/shard_map/cond/branch_1_fun/ppermute | solution.py:177
  92.2 32.9 %copy-start.1 = (f32[512,128]{1,0:T(8,128)S(1)}, f32[512,128]{1,0:T(8,128)}, u32[]{:S(2)}) copy-start(f32[512,128]{1,0:T(8,128)} %frag_ref.1) | copy-start | bytes 786436
  92.2 32.9 %copy-start.2 = (f32[512,128]{1,0:T(8,128)S(1)}, f32[512,128]{1,0:T(8,128)}, u32[]{:S(2)}) copy-start(f32[512,128]{1,0:T(8,128)} %mom_ref.1) | copy-start | bytes 786436
  92.2 31.9 %collective-permute-start.11 = (bf16[512,128]{1,0:T(8,128)(2,1)S(1)}, bf16[512,128]{1,0:T(8,128)(2,1)S(1)}, u32[]{:S(2)}, u32[]{:S(2)}) collective-permute-start(bf16[512,128]{1,0:T(8,128)(2,1)S(1)} %join.1.ours_ref), channel_id=1, source_target_pairs={{0,16},{16,0},{32,48},{48,32},{64,80},{80,64},{96,112},{112,96},{1... | collective-permute-start | bytes 393224 | tf_op jit(solution)/shard_map/ppermute | solution.py:181
  116.1 10.8 %copy-start.6 = (bf16[128,512]{1,0:T(8,128)(2,1)}, bf16[128,512]{1,0:T(8,128)(2,1)S(1)}, u32[]{:S(2)}) copy-start(bf16[128,512]{1,0:T(8,128)(2,1)S(1)} %get-tuple-element.87) | copy-start | bytes 393220

commit v4 on v3

--- a/solution.py
+++ b/solution.py
@@ -28,7 +28,9 @@
 ALONG_Z = [[x * 8 + z for z in range(8)] for x in range(4)]
 ACROSS = [(f, f ^ HALF) for f in range(PARTS)]
 
-TOK = 32
+TOK = 64
+LANES = 128
+NORM_VMEM = 60 * 1024 * 1024
 NEAR = 0
 FAR = BLOCK
 COT = 2 * BLOCK
@@ -36,16 +38,24 @@
 
 
 def norm_kernel(half_ref, acts_ref, gain_ref, cot_ref, out_ref):
-    half = half_ref[0]
     rows = acts_ref[...].astype(jnp.float32)
     scale = lax.rsqrt(jnp.mean(rows * rows, axis=-1, keepdims=True) + 1e-05)
+    gain = gain_ref[...].astype(jnp.float32)
     cot = cot_ref[...]
     span = HALF * BLOCK
+    for half in range(2):
+
+        @pl.when(half_ref[0] == half)
+        def _():
+            for which, slot in ((half, NEAR), (1 - half, FAR)):
+                for j in range(HALF):
+                    for k in range(0, BLOCK, LANES):
+                        start = which * span + j * BLOCK + k
+                        row = start // LANES
+                        part = acts_ref[:, start : start + LANES].astype(jnp.float32) * scale * gain[row : row + 1, :]
+                        out_ref[j, :, slot + k : slot + k + LANES] = part.astype(jnp.bfloat16)
+
     for j in range(HALF):
-        for which, slot in ((half, NEAR), (1 - half, FAR)):
-            at = pl.ds(pl.multiple_of(which * span + j * BLOCK, BLOCK), BLOCK)
-            part = acts_ref[:, at].astype(jnp.float32) * scale * gain_ref[:, at].astype(jnp.float32)
-            out_ref[j, :, slot : slot + BLOCK] = part.astype(jnp.bfloat16)
         out_ref[j, :, COT : COT + KVW] = cot
 
 
@@ -57,13 +67,13 @@
             grid=(ROWS_IN // TOK,),
             in_specs=[
                 pl.BlockSpec((TOK, D), lambda i, h: (i, 0)),
-                pl.BlockSpec((1, D), lambda i, h: (0, 0)),
+                pl.BlockSpec((D // LANES, LANES), lambda i, h: (0, 0)),
                 pl.BlockSpec((TOK, KVW), lambda i, h: (i, 0)),
             ],
             out_specs=pl.BlockSpec((HALF, TOK, WIDE), lambda i, h: (0, i, 0)),
         ),
         out_shape=jax.ShapeDtypeStruct((HALF, ROWS_IN, WIDE), jnp.bfloat16),
-        compiler_params=pltpu.CompilerParams(vmem_limit_bytes=32 * 1024 * 1024),
+        compiler_params=pltpu.CompilerParams(vmem_limit_bytes=NORM_VMEM),
         cost_estimate=SHORT,
         name="normalise",
     )(half, acts, gain, cot)
@@ -73,11 +83,11 @@
     return lax.dot_general(left, right, (((0,), (0,)), ((), ())), preferred_element_type=jnp.float32)
 
 
-def far_kernel(normed_ref, cot_ref, out_ref):
+def far_kernel(normed_ref, cot_ref, _, out_ref):
     out_ref[...] = (transposed_dot(normed_ref[...], cot_ref[...]) * INV_ROOT).astype(jnp.bfloat16)
 
 
-def far_gradient(mixed):
+def far_gradient(mixed, after):
     tokens = mixed.shape[0]
     step = 256
     return pl.pallas_call(
@@ -86,13 +96,14 @@
         in_specs=[
             pl.BlockSpec((tokens, step), lambda i: (0, FAR // step + i)),
             pl.BlockSpec((tokens, KVW), lambda i: (0, COT // KVW)),
+            pl.BlockSpec(memory_space=pl.ANY),
         ],
         out_specs=pl.BlockSpec((step, KVW), lambda i: (i, 0)),
         out_shape=jax.ShapeDtypeStruct((BLOCK, KVW), jnp.bfloat16),
         compiler_params=pltpu.CompilerParams(vmem_limit_bytes=32 * 1024 * 1024),
         cost_estimate=SHORT,
         name="far_gradient",
-    )(mixed, mixed)
+    )(mixed, mixed, after)
 
 
 def near_kernel(mixed_ref, near_weight_ref, far_weight_ref, keys_ref, stepped_ref):
@@ -136,23 +147,16 @@
 
 
 def blend(start, stepped, arrived, ours, theirs, frag, mom):
-    step = 128
-    wide = pl.BlockSpec((step, KVW), lambda i, s: (i, 0))
-    slim = pl.BlockSpec((step, HD), lambda i, s: (i, 0))
     return pl.pallas_call(
         blend_kernel,
-        grid_spec=pltpu.PrefetchScalarGridSpec(
-            num_scalar_prefetch=1,
-            grid=(BLOCK // step,),
-            in_specs=[wide, wide, slim, slim, slim, slim],
-            out_specs=[wide, slim, slim],
-        ),
+        in_specs=[pl.BlockSpec(memory_space=pltpu.SMEM)] + [pl.BlockSpec(memory_space=pltpu.VMEM)] * 6,
+        out_specs=[pl.BlockSpec(memory_space=pltpu.VMEM)] * 3,
         out_shape=[
             jax.ShapeDtypeStruct((BLOCK, KVW), jnp.bfloat16),
             jax.ShapeDtypeStruct((BLOCK, HD), jnp.float32),
             jax.ShapeDtypeStruct((BLOCK, HD), jnp.float32),
         ],
-        compiler_params=pltpu.CompilerParams(vmem_limit_bytes=32 * 1024 * 1024),
+        compiler_params=pltpu.CompilerParams(vmem_limit_bytes=24 * 1024 * 1024),
         name="blend",
     )(start, stepped, arrived, ours, theirs, frag, mom)
 
@@ -202,9 +206,10 @@
 def hold(rows):
     return pl.pallas_call(
         hold_kernel,
-        out_shape=jax.ShapeDtypeStruct(rows.shape, rows.dtype),
-        in_specs=[pl.BlockSpec(memory_space=pltpu.VMEM)],
-        out_specs=pl.BlockSpec(memory_space=pltpu.VMEM),
+        grid=(1,),
+        in_specs=[pl.BlockSpec((16, LANES), lambda i: (0, 0))],
+        out_specs=pl.BlockSpec((16, LANES), lambda i: (0, 0)),
+        out_shape=jax.ShapeDtypeStruct((16, LANES), rows.dtype),
         compiler_params=pltpu.CompilerParams(vmem_limit_bytes=16 * 1024 * 1024),
         cost_estimate=HOLD_COST,
         name="hold",
@@ -247,14 +252,12 @@
     far_weight = lax.ppermute(weight, "fsdp", ACROSS)
 
     half = (lax.axis_index("fsdp") // HALF).astype(jnp.int32).reshape(1)
-    mixed = normalise(half, acts, norm_gain.reshape(1, D), key_cotangent)
+    mixed = normalise(half, acts, norm_gain.reshape(D // LANES, LANES), key_cotangent)
     delta, mixed = lax.optimization_barrier((pending_delta[0], mixed))
     mixed = exchange(mixed.reshape(HALF * ROWS_IN, WIDE), "fsdp", HALVES)
     own = staged(go, reduce_x, delta)
     arrivals = [paired(own, bits) for bits in (2, 4, 6)]
-    far_weight = hold(far_weight)
-    mixed, far_weight = lax.optimization_barrier((mixed, far_weight))
-    sent = far_gradient(mixed)
+    sent = far_gradient(mixed, hold(far_weight))
     arrived = lax.ppermute(sent, "fsdp", ACROSS)
 
     def second(mixed, own, arrivals, weight, far_weight):

time: 128 us -> 127 us (level)
  the two profiles are of different devices: /device:TPU:34 before, /device:TPU:64 now
where the time goes in v4:
time: 127 us; the launch traced here: 126 us
  starting transfers between devices  71.3 us (56%)
  blocking collectives  20.5 us (16%)
  waiting for transfers between devices  16.9 us (13%)
  Pallas kernels  12 us (9%)
  other arithmetic  2.03 us (2%)
  local copies, waits for them, and re-layouts  1.68 us (1%)
  between operations  1.48 us (1%)
    ppermute x6, starting transfers between devices, turned(): return lax.ppermute(rows, 'replica', ring)  22.8 us
    all_to_all x1, blocking collectives, exchange(): lax.all_to_all(rows, axis, split_axis=0, concat_axis=0, tiled=True, axis_...  20.5 us
    ppermute x1, starting transfers between devices, body(): arrived = lax.ppermute(sent, 'fsdp', ACROSS)  15.7 us
    ppermute x4, starting transfers between devices, paired(): lax.ppermute(rows, 'replica', [(r, r ^ bits) for r in range(REPLICAS)])  14.3 us
    ppermute x1, starting transfers between devices, body(): far_weight = lax.ppermute(weight, 'fsdp', ACROSS)  13.9 us
    all_to_all x1, waiting for transfers between devices, exchange(): lax.all_to_all(rows, axis, split_axis=0, concat_axis=0, tiled=True, axis_...  10.8 us
    all_to_all x1, starting transfers between devices, exchange(): lax.all_to_all(rows, axis, split_axis=0, concat_axis=0, tiled=True, axis_...  4.6 us
    pallas_call x1, Pallas kernels, normalise(): pl.pallas_call(norm_kernel, grid_spec=pltpu.PrefetchScalarGridSpec(num_sc...  3.7 us
  transfers between devices with their start and end apart: 13, of which 3 were waited for; matrix products, arithmetic and copies ran while one was open for 2% of the time, Pallas kernels for 8%

profile of v4, /device:TPU:64, one launch (start us, length us, event | category | flops | bytes accessed | tf_op | source)
XLA Modules:
  0.0 126.1 jit_solution(11158529912057939552)
XLA Ops:
  0.6 13.9 %collective-permute-start.6 = (bf16[512,512]{1,0:T(8,128)(2,1)}, bf16[512,512]{1,0:T(8,128)(2,1)}, u32[]{:S(2)}, u32[]{:S(2)}) collective-permute-start(bf16[512,512]{1,0:T(8,128)(2,1)} %bitcast.13), channel_id=1, source_target_pairs={{0,8},{1,9},{2,10},{3,11},{4,12},{5,13},{6,14},{7,15},{8,0},{9,1},... | collective-permute-start | bytes 1572872 | tf_op jit(solution)/shard_map/ppermute | solution.py:252
  14.6 3.7 %normalise.1 = bf16[8,128,1536]{2,1,0:T(8,128)(2,1)} custom-call(s32[1]{0:T(128)} %bitcast.3.half_ref, bf16[128,8192]{1,0:T(8,128)(2,1)} %acts_ref.1, bf16[64,128]{1,0:T(8,128)(2,1)} %bitcast.16, bf16[128,512]{1,0:T(8,128)(2,1)} %cot_ref.1), custom_call_target="tpu_custom_call" | custom-call | flops 1000000 | bytes 10000 | tf_op jit(solution)/shard_map/normalise/pallas_call | solution.py:63
  18.3 4.6 %all-to-all-start.1 = ((bf16[8,128,1536]{2,1,0:T(8,128)(2,1)}), bf16[8,128,1536]{2,1,0:T(8,128)(2,1)S(1)}, u32[]{:S(2)}, u32[]{:S(2)}) async-start(bf16[8,128,1536]{2,1,0:T(8,128)(2,1)} %normalise.1), calls=%async_computation.1 | async-start | bytes 6291456 | tf_op jit(solution)/shard_map/all_to_all | solution.py:171
  23.6 14.0 %conditional.3 = (bf16[128,128]{1,0:T(8,128)(2,1)S(1)}) conditional(s32[]{:T(128)} %bitcast.1, () %tuple.34, bf16[512,128]{1,0:T(8,128)(2,1)S(1)} %bitcast.15), branch_computations={%region_0.1_spmd, %region_1.2_spmd} | conditional | flops 131133 | bytes 754462 | solution.py:167
  23.7 3.4 %collective-permute-start = (bf16[128,128]{1,0:T(8,128)(2,1)S(1)}, bf16[128,128]{1,0:T(8,128)(2,1)S(1)}, u32[]{:S(2)}, u32[]{:S(2)}) collective-permute-start(bf16[128,128]{1,0:T(8,128)(2,1)S(1)} %get-tuple-element.67), channel_id=1, source_target_pairs={{0,128},{16,144},{32,160},{48,176},{64,192},{80,208},{96,224},{112... | collective-permute-start | bytes 98312 | tf_op jit(solution)/shard_map/cond/branch_1_fun/ppermute | solution.py:181
  27.1 4.6 %collective-permute-start.1 = (bf16[128,128]{1,0:T(8,128)(2,1)S(1)}, bf16[128,128]{1,0:T(8,128)(2,1)S(1)}, u32[]{:S(2)}, u32[]{:S(2)}) collective-permute-start(bf16[128,128]{1,0:T(8,128)(2,1)S(1)} %get-tuple-element.69), channel_id=1, source_target_pairs={{0,256},{16,272},{32,288},{48,304},{64,320},{80,336},{96,352},{112... | collective-permute-start | bytes 98312 | tf_op jit(solution)/shard_map/cond/branch_1_fun/ppermute | solution.py:181
  31.7 3.3 %collective-permute-start.2 = (bf16[128,128]{1,0:T(8,128)(2,1)S(1)}, bf16[128,128]{1,0:T(8,128)(2,1)S(1)}, u32[]{:S(2)}, u32[]{:S(2)}) collective-permute-start(bf16[128,128]{1,0:T(8,128)(2,1)S(1)} %get-tuple-element.68), channel_id=1, source_target_pairs={{0,384},{16,400},{32,416},{48,432},{64,448},{80,464},{96,480},{112... | collective-permute-start | bytes 98312 | tf_op jit(solution)/shard_map/cond/branch_1_fun/ppermute | solution.py:181
  35.1 2.4 %collective-permute-done.2 = bf16[128,128]{1,0:T(8,128)(2,1)S(1)} collective-permute-done((bf16[128,128]{1,0:T(8,128)(2,1)S(1)}, bf16[128,128]{1,0:T(8,128)(2,1)S(1)}, u32[]{:S(2)}, u32[]{:S(2)}) %collective-permute-start.2) | collective-permute-done | bytes 32800 | tf_op jit(solution)/shard_map/cond/branch_1_fun/ppermute | solution.py:181
  37.5 3.4 %collective-permute-start.7 = (bf16[128,128]{1,0:T(8,128)(2,1)S(1)}, bf16[128,128]{1,0:T(8,128)(2,1)S(1)}, u32[]{:S(2)}, u32[]{:S(2)}) collective-permute-start(bf16[128,128]{1,0:T(8,128)(2,1)S(1)} %get-tuple-element.82), channel_id=1, source_target_pairs={{0,32},{16,48},{32,0},{48,16},{64,96},{80,112},{96,64},{112,80},{1... | collective-permute-start | bytes 98312 | tf_op jit(solution)/shard_map/ppermute | solution.py:185
  40.9 4.3 %collective-permute-start.8 = (bf16[128,128]{1,0:T(8,128)(2,1)S(1)}, bf16[128,128]{1,0:T(8,128)(2,1)S(1)}, u32[]{:S(2)}, u32[]{:S(2)}) collective-permute-start(bf16[128,128]{1,0:T(8,128)(2,1)S(1)} %get-tuple-element.82), channel_id=1, source_target_pairs={{0,64},{16,80},{32,96},{48,112},{64,0},{80,16},{96,32},{112,48},{1... | collective-permute-start | bytes 98312 | tf_op jit(solution)/shard_map/ppermute | solution.py:185
  45.2 4.6 %collective-permute-start.9 = (bf16[128,128]{1,0:T(8,128)(2,1)S(1)}, bf16[128,128]{1,0:T(8,128)(2,1)S(1)}, u32[]{:S(2)}, u32[]{:S(2)}) collective-permute-start(bf16[128,128]{1,0:T(8,128)(2,1)S(1)} %get-tuple-element.82), channel_id=1, source_target_pairs={{0,96},{16,112},{32,64},{48,80},{64,32},{80,48},{96,0},{112,16},{1... | collective-permute-start | bytes 98312 | tf_op jit(solution)/shard_map/ppermute | solution.py:185
  49.8 0.7 hold.1._
  50.5 10.8 %all-to-all-done.1 = bf16[8,128,1536]{2,1,0:T(8,128)(2,1)S(1)} async-done(((bf16[8,128,1536]{2,1,0:T(8,128)(2,1)}), bf16[8,128,1536]{2,1,0:T(8,128)(2,1)S(1)}, u32[]{:S(2)}, u32[]{:S(2)}) %all-to-all-start.1) | async-done | bytes 3145760 | tf_op jit(solution)/shard_map/all_to_all | solution.py:171
  61.3 1.6 %copy-done.2 = bf16[8,128,1536]{2,1,0:T(8,128)(2,1)} copy-done((bf16[8,128,1536]{2,1,0:T(8,128)(2,1)}, bf16[8,128,1536]{2,1,0:T(8,128)(2,1)S(1)}, u32[]{:S(2)}) %copy-start.2) | copy-done | bytes 3145752
  63.0 2.5 %far_gradient.1 = bf16[512,512]{1,0:T(8,128)(2,1)S(1)} custom-call(bf16[1024,1536]{1,0:T(8,128)(2,1)} %bitcast.9, bf16[1024,1536]{1,0:T(8,128)(2,1)} %bitcast.10, bf16[16,128]{1,0:T(8,128)(2,1)S(1)} %hold.1._), custom_call_target="tpu_custom_call" | custom-call | flops 1000000 | bytes 10000 | tf_op jit(solution)/shard_map/far_gradient/pallas_call | solution.py:93
  65.5 15.7 %collective-permute-start.10 = (bf16[512,512]{1,0:T(8,128)(2,1)S(1)}, bf16[512,512]{1,0:T(8,128)(2,1)S(1)}, u32[]{:S(2)}, u32[]{:S(2)}) collective-permute-start(bf16[512,512]{1,0:T(8,128)(2,1)S(1)} %far_gradient.1), channel_id=1, source_target_pairs={{0,8},{1,9},{2,10},{3,11},{4,12},{5,13},{6,14},{7,15},{8,0},{9,1},... | collective-permute-start | bytes 1572872 | tf_op jit(solution)/shard_map/ppermute | solution.py:261
  81.3 15.0 %conditional.4 = (bf16[1024,512]{1,0:T(8,128)(2,1)S(1)}, f32[512,512]{1,0:T(8,128)S(1)}, bf16[128,128]{1,0:T(8,128)(2,1)}, bf16[128,128]{1,0:T(8,128)(2,1)}, bf1...) conditional(s32[]{:T(128)} %bitcast.1, () %tuple.32, (bf16[1024,1536]{1,0:T(8,128)(2,1)S(1)}, ...), branch_computations={%region_2.3_spmd, %region_3.4_spmd} | conditional | flops 131072 | bytes 2228286 | solution.py:167
  81.3 0.6 add_convert_fusion.1
  81.9 1.9 %collective-permute-start.3 = (bf16[128,128]{1,0:T(8,128)(2,1)}, bf16[128,128]{1,0:T(8,128)(2,1)}, u32[]{:S(2)}, u32[]{:S(2)}) collective-permute-start(bf16[128,128]{1,0:T(8,128)(2,1)} %add_convert_fusion.1), channel_id=1, source_target_pairs={{0,128},{16,144},{32,160},{48,176},{64,192},{80,208},{96,224},{112... | collective-permute-start | bytes 98312 | tf_op jit(solution)/shard_map/cond/branch_1_fun/ppermute | solution.py:181
  83.8 6.1 %collective-permute-start.4 = (bf16[128,128]{1,0:T(8,128)(2,1)}, bf16[128,128]{1,0:T(8,128)(2,1)}, u32[]{:S(2)}, u32[]{:S(2)}) collective-permute-start(bf16[128,128]{1,0:T(8,128)(2,1)} %add_convert_fusion.1), channel_id=1, source_target_pairs={{0,256},{16,272},{32,288},{48,304},{64,320},{80,336},{96,352},{112... | collective-permute-start | bytes 98312 | tf_op jit(solution)/shard_map/cond/branch_1_fun/ppermute | solution.py:181
  90.0 3.4 %collective-permute-start.5 = (bf16[128,128]{1,0:T(8,128)(2,1)}, bf16[128,128]{1,0:T(8,128)(2,1)}, u32[]{:S(2)}, u32[]{:S(2)}) collective-permute-start(bf16[128,128]{1,0:T(8,128)(2,1)} %add_convert_fusion.1), channel_id=1, source_target_pairs={{0,384},{16,400},{32,416},{48,432},{64,448},{80,464},{96,480},{112... | collective-permute-start | bytes 98312 | tf_op jit(solution)/shard_map/cond/branch_1_fun/ppermute | solution.py:181
  93.4 2.8 %near_work.1 = (bf16[1024,512]{1,0:T(8,128)(2,1)S(1)}, f32[512,512]{1,0:T(8,128)S(1)}) custom-call(bf16[1024,1536]{1,0:T(8,128)(2,1)S(1)} %get-tuple-element.22.mixed_ref, bf16[512,512]{1,0:T(8,128)(2,1)S(1)} %get-tuple-element.23.near_weight_ref, bf16[512,512]{1,0:T(8,128)(2,1)} %get-tuple-element.24.far_weight_ref), custom_call_target="tpu_custom_call" | custom-call | tf_op jit(solution)/shard_map/cond/branch_1_fun/near_work/pallas_call | solution.py:120
  96.2 0.8 join.1.ours_ref
  97.1 0.0 copy-start
  97.1 0.0 copy-start.1
  97.1 2.1 %collective-permute-start.11 = (bf16[512,128]{1,0:T(8,128)(2,1)S(1)}, bf16[512,128]{1,0:T(8,128)(2,1)S(1)}, u32[]{:S(2)}, u32[]{:S(2)}) collective-permute-start(bf16[512,128]{1,0:T(8,128)(2,1)S(1)} %join.1.ours_ref), channel_id=1, source_target_pairs={{0,16},{16,0},{32,48},{48,32},{64,80},{80,64},{96,112},{112,96},{1... | collective-permute-start | bytes 393224 | tf_op jit(solution)/shard_map/ppermute | solution.py:185
  99.1 21.9 %conditional.5 = (bf16[128,512]{1,0:T(8,128)(2,1)S(1)}) conditional(s32[]{:T(128)} %bitcast.1, () %tuple.31, bf16[1024,512]{1,0:T(8,128)(2,1)S(1)} %get-tuple-element.58), branch_computations={%region_4.5_spmd, %region_5.7_spmd} | conditional | flops 458752 | bytes 3276810 | solution.py:167
  99.2 20.5 %all_to_all.15 = bf16[8,128,512]{2,1,0:T(8,128)(2,1)} all-to-all(bf16[8,128,512]{2,1,0:T(8,128)(2,1)S(1)} %bitcast.12), channel_id=1, replica_groups={{0,1,2,3,4,5,6,7},{8,9,10,11,12,13,14,15},{16,17,18,19,20,21,22,23},{24..., dimensions={0} | all-to-all | bytes 2097152 | tf_op jit(solution)/shard_map/cond/branch_1_fun/all_to_all | solution.py:171
  119.6 1.4 %reduce_sum.11 = bf16[128,512]{1,0:T(8,128)(2,1)S(1)} reduce(bf16[8,128,512]{2,1,0:T(8,128)(2,1)} %all_to_all.15, bf16[]{:T(256)} %constant.75.clone), dimensions={0}, to_apply=%region_6.6 | reduce | flops 458752 | bytes 1179650 | tf_op jit(solution)/shard_map/cond/branch_1_fun/reduce_sum | solution.py:176
  121.0 0.0 copy-start.6
  121.0 3.6 %collective-permute-done.10.arrived_ref = bf16[512,512]{1,0:T(8,128)(2,1)S(1)} collective-permute-done((bf16[512,512]{1,0:T(8,128)(2,1)S(1)}, bf16[512,512]{1,0:T(8,128)(2,1)S(1)}, u32[]{:S(2)}, u32[]{:S(2)}) %collective-permute-start.10) | collective-permute-done | bytes 524320 | tf_op jit(solution)/shard_map/ppermute | solution.py:261
  124.7 1.4 %blend.1 = (bf16[512,512]{1,0:T(8,128)(2,1)}, f32[512,128]{1,0:T(8,128)}, f32[512,128]{1,0:T(8,128)}) custom-call(s32[1]{0:T(128)S(6)} %copy.28.start_ref, f32[512,512]{1,0:T(8,128)S(1)} %get-tuple-element.61.stepped_ref, bf16[512,512]{1,0:T(8,128)(2,1)S(1)} %collective-permute-done.10.arrived_ref, bf16[512,128]{1,0:T(8,128)(2,1)S(1)} %join.1.ours_ref, ...), custom_call_target="tpu_custom_call" | custom-call | tf_op jit(solution)/shard_map/blend/pallas_call | solution.py:150
  (22 shorter events, 0.1 us)
Async XLA Ops:
  0.6 49.2 %collective-permute-start.6 = (bf16[512,512]{1,0:T(8,128)(2,1)}, bf16[512,512]{1,0:T(8,128)(2,1)}, u32[]{:S(2)}, u32[]{:S(2)}) collective-permute-start(bf16[512,512]{1,0:T(8,128)(2,1)} %bitcast.13), channel_id=1, source_target_pairs={{0,8},{1,9},{2,10},{3,11},{4,12},{5,13},{6,14},{7,15},{8,0},{9,1},... | collective-permute-start | bytes 1572872 | tf_op jit(solution)/shard_map/ppermute | solution.py:252
  18.3 5.3 %copy-start.5 = (bf16[1,512,128]{2,1,0:T(8,128)(2,1)S(1)}, bf16[1,512,128]{2,1,0:T(8,128)(2,1)}, u32[]{:S(2)}) copy-start(bf16[1,512,128]{2,1,0:T(8,128)(2,1)} %param.18) | copy-start | bytes 393220
  18.3 43.0 %all-to-all-start.1 = ((bf16[8,128,1536]{2,1,0:T(8,128)(2,1)}), bf16[8,128,1536]{2,1,0:T(8,128)(2,1)S(1)}, u32[]{:S(2)}, u32[]{:S(2)}) async-start(bf16[8,128,1536]{2,1,0:T(8,128)(2,1)} %normalise.1), calls=%async_computation.1 | async-start | bytes 6291456 | tf_op jit(solution)/shard_map/all_to_all | solution.py:171
  23.7 11.4 %collective-permute-start = (bf16[128,128]{1,0:T(8,128)(2,1)S(1)}, bf16[128,128]{1,0:T(8,128)(2,1)S(1)}, u32[]{:S(2)}, u32[]{:S(2)}) collective-permute-start(bf16[128,128]{1,0:T(8,128)(2,1)S(1)} %get-tuple-element.67), channel_id=1, source_target_pairs={{0,128},{16,144},{32,160},{48,176},{64,192},{80,208},{96,224},{112... | collective-permute-start | bytes 98312 | tf_op jit(solution)/shard_map/cond/branch_1_fun/ppermute | solution.py:181
  27.1 8.0 %collective-permute-start.1 = (bf16[128,128]{1,0:T(8,128)(2,1)S(1)}, bf16[128,128]{1,0:T(8,128)(2,1)S(1)}, u32[]{:S(2)}, u32[]{:S(2)}) collective-permute-start(bf16[128,128]{1,0:T(8,128)(2,1)S(1)} %get-tuple-element.69), channel_id=1, source_target_pairs={{0,256},{16,272},{32,288},{48,304},{64,320},{80,336},{96,352},{112... | collective-permute-start | bytes 98312 | tf_op jit(solution)/shard_map/cond/branch_1_fun/ppermute | solution.py:181
  31.7 5.8 %collective-permute-start.2 = (bf16[128,128]{1,0:T(8,128)(2,1)S(1)}, bf16[128,128]{1,0:T(8,128)(2,1)S(1)}, u32[]{:S(2)}, u32[]{:S(2)}) collective-permute-start(bf16[128,128]{1,0:T(8,128)(2,1)S(1)} %get-tuple-element.68), channel_id=1, source_target_pairs={{0,384},{16,400},{32,416},{48,432},{64,448},{80,464},{96,480},{112... | collective-permute-start | bytes 98312 | tf_op jit(solution)/shard_map/cond/branch_1_fun/ppermute | solution.py:181
  37.5 43.7 %collective-permute-start.7 = (bf16[128,128]{1,0:T(8,128)(2,1)S(1)}, bf16[128,128]{1,0:T(8,128)(2,1)S(1)}, u32[]{:S(2)}, u32[]{:S(2)}) collective-permute-start(bf16[128,128]{1,0:T(8,128)(2,1)S(1)} %get-tuple-element.82), channel_id=1, source_target_pairs={{0,32},{16,48},{32,0},{48,16},{64,96},{80,112},{96,64},{112,80},{1... | collective-permute-start | bytes 98312 | tf_op jit(solution)/shard_map/ppermute | solution.py:185
  40.9 40.3 %collective-permute-start.8 = (bf16[128,128]{1,0:T(8,128)(2,1)S(1)}, bf16[128,128]{1,0:T(8,128)(2,1)S(1)}, u32[]{:S(2)}, u32[]{:S(2)}) collective-permute-start(bf16[128,128]{1,0:T(8,128)(2,1)S(1)} %get-tuple-element.82), channel_id=1, source_target_pairs={{0,64},{16,80},{32,96},{48,112},{64,0},{80,16},{96,32},{112,48},{1... | collective-permute-start | bytes 98312 | tf_op jit(solution)/shard_map/ppermute | solution.py:185
  45.2 36.0 %collective-permute-start.9 = (bf16[128,128]{1,0:T(8,128)(2,1)S(1)}, bf16[128,128]{1,0:T(8,128)(2,1)S(1)}, u32[]{:S(2)}, u32[]{:S(2)}) collective-permute-start(bf16[128,128]{1,0:T(8,128)(2,1)S(1)} %get-tuple-element.82), channel_id=1, source_target_pairs={{0,96},{16,112},{32,64},{48,80},{64,32},{80,48},{96,0},{112,16},{1... | collective-permute-start | bytes 98312 | tf_op jit(solution)/shard_map/ppermute | solution.py:185
  61.3 1.6 %copy-start.2 = (bf16[8,128,1536]{2,1,0:T(8,128)(2,1)}, bf16[8,128,1536]{2,1,0:T(8,128)(2,1)S(1)}, u32[]{:S(2)}) copy-start(bf16[8,128,1536]{2,1,0:T(8,128)(2,1)S(1)} %all-to-all-done.1) | copy-start | bytes 9437188
  63.0 18.3 %copy-start.3 = (bf16[8,128,1536]{2,1,0:T(8,128)(2,1)S(1)}, bf16[8,128,1536]{2,1,0:T(8,128)(2,1)}, u32[]{:S(2)}) copy-start(bf16[8,128,1536]{2,1,0:T(8,128)(2,1)} %copy-done.2) | copy-start | bytes 9437188
  63.0 18.3 %copy-start.4 = (bf16[1,512,512]{2,1,0:T(8,128)(2,1)S(1)}, bf16[1,512,512]{2,1,0:T(8,128)(2,1)}, u32[]{:S(2)}) copy-start(bf16[1,512,512]{2,1,0:T(8,128)(2,1)} %param.16) | copy-start | bytes 1572868
  65.5 59.2 %collective-permute-start.10 = (bf16[512,512]{1,0:T(8,128)(2,1)S(1)}, bf16[512,512]{1,0:T(8,128)(2,1)S(1)}, u32[]{:S(2)}, u32[]{:S(2)}) collective-permute-start(bf16[512,512]{1,0:T(8,128)(2,1)S(1)} %far_gradient.1), channel_id=1, source_target_pairs={{0,8},{1,9},{2,10},{3,11},{4,12},{5,13},{6,14},{7,15},{8,0},{9,1},... | collective-permute-start | bytes 1572872 | tf_op jit(solution)/shard_map/ppermute | solution.py:261
  81.9 14.3 %collective-permute-start.3 = (bf16[128,128]{1,0:T(8,128)(2,1)}, bf16[128,128]{1,0:T(8,128)(2,1)}, u32[]{:S(2)}, u32[]{:S(2)}) collective-permute-start(bf16[128,128]{1,0:T(8,128)(2,1)} %add_convert_fusion.1), channel_id=1, source_target_pairs={{0,128},{16,144},{32,160},{48,176},{64,192},{80,208},{96,224},{112... | collective-permute-start | bytes 98312 | tf_op jit(solution)/shard_map/cond/branch_1_fun/ppermute | solution.py:181
  83.8 12.4 %collective-permute-start.4 = (bf16[128,128]{1,0:T(8,128)(2,1)}, bf16[128,128]{1,0:T(8,128)(2,1)}, u32[]{:S(2)}, u32[]{:S(2)}) collective-permute-start(bf16[128,128]{1,0:T(8,128)(2,1)} %add_convert_fusion.1), channel_id=1, source_target_pairs={{0,256},{16,272},{32,288},{48,304},{64,320},{80,336},{96,352},{112... | collective-permute-start | bytes 98312 | tf_op jit(solution)/shard_map/cond/branch_1_fun/ppermute | solution.py:181
  90.0 6.3 %collective-permute-start.5 = (bf16[128,128]{1,0:T(8,128)(2,1)}, bf16[128,128]{1,0:T(8,128)(2,1)}, u32[]{:S(2)}, u32[]{:S(2)}) collective-permute-start(bf16[128,128]{1,0:T(8,128)(2,1)} %add_convert_fusion.1), channel_id=1, source_target_pairs={{0,384},{16,400},{32,416},{48,432},{64,448},{80,464},{96,480},{112... | collective-permute-start | bytes 98312 | tf_op jit(solution)/shard_map/cond/branch_1_fun/ppermute | solution.py:181
  97.1 27.6 %copy-start = (f32[512,128]{1,0:T(8,128)S(1)}, f32[512,128]{1,0:T(8,128)}, u32[]{:S(2)}) copy-start(f32[512,128]{1,0:T(8,128)} %frag_ref.1) | copy-start | bytes 786436
  97.1 27.6 %copy-start.1 = (f32[512,128]{1,0:T(8,128)S(1)}, f32[512,128]{1,0:T(8,128)}, u32[]{:S(2)}) copy-start(f32[512,128]{1,0:T(8,128)} %mom_ref.1) | copy-start | bytes 786436
  97.1 24.0 %collective-permute-start.11 = (bf16[512,128]{1,0:T(8,128)(2,1)S(1)}, bf16[512,128]{1,0:T(8,128)(2,1)S(1)}, u32[]{:S(2)}, u32[]{:S(2)}) collective-permute-start(bf16[512,128]{1,0:T(8,128)(2,1)S(1)} %join.1.ours_ref), channel_id=1, source_target_pairs={{0,16},{16,0},{32,48},{48,32},{64,80},{80,64},{96,112},{112,96},{1... | collective-permute-start | bytes 393224 | tf_op jit(solution)/shard_map/ppermute | solution.py:185
  121.0 5.1 %copy-start.6 = (bf16[128,512]{1,0:T(8,128)(2,1)}, bf16[128,512]{1,0:T(8,128)(2,1)S(1)}, u32[]{:S(2)}) copy-start(bf16[128,512]{1,0:T(8,128)(2,1)S(1)} %get-tuple-element.83) | copy-start | bytes 393220

commit v5 on v4

--- a/solution.py
+++ b/solution.py
@@ -83,11 +83,11 @@
     return lax.dot_general(left, right, (((0,), (0,)), ((), ())), preferred_element_type=jnp.float32)
 
 
-def far_kernel(normed_ref, cot_ref, _, out_ref):
+def far_kernel(normed_ref, cot_ref, out_ref):
     out_ref[...] = (transposed_dot(normed_ref[...], cot_ref[...]) * INV_ROOT).astype(jnp.bfloat16)
 
 
-def far_gradient(mixed, after):
+def far_gradient(mixed):
     tokens = mixed.shape[0]
     step = 256
     return pl.pallas_call(
@@ -96,14 +96,13 @@
         in_specs=[
             pl.BlockSpec((tokens, step), lambda i: (0, FAR // step + i)),
             pl.BlockSpec((tokens, KVW), lambda i: (0, COT // KVW)),
-            pl.BlockSpec(memory_space=pl.ANY),
         ],
         out_specs=pl.BlockSpec((step, KVW), lambda i: (i, 0)),
         out_shape=jax.ShapeDtypeStruct((BLOCK, KVW), jnp.bfloat16),
         compiler_params=pltpu.CompilerParams(vmem_limit_bytes=32 * 1024 * 1024),
         cost_estimate=SHORT,
         name="far_gradient",
-    )(mixed, mixed, after)
+    )(mixed, mixed)
 
 
 def near_kernel(mixed_ref, near_weight_ref, far_weight_ref, keys_ref, stepped_ref):
@@ -206,10 +205,9 @@
 def hold(rows):
     return pl.pallas_call(
         hold_kernel,
-        grid=(1,),
-        in_specs=[pl.BlockSpec((16, LANES), lambda i: (0, 0))],
-        out_specs=pl.BlockSpec((16, LANES), lambda i: (0, 0)),
-        out_shape=jax.ShapeDtypeStruct((16, LANES), rows.dtype),
+        out_shape=jax.ShapeDtypeStruct(rows.shape, rows.dtype),
+        in_specs=[pl.BlockSpec(memory_space=pltpu.VMEM)],
+        out_specs=pl.BlockSpec(memory_space=pltpu.VMEM),
         compiler_params=pltpu.CompilerParams(vmem_limit_bytes=16 * 1024 * 1024),
         cost_estimate=HOLD_COST,
         name="hold",
@@ -256,8 +254,10 @@
     delta, mixed = lax.optimization_barrier((pending_delta[0], mixed))
     mixed = exchange(mixed.reshape(HALF * ROWS_IN, WIDE), "fsdp", HALVES)
     own = staged(go, reduce_x, delta)
-    arrivals = [paired(own, bits) for bits in (2, 4, 6)]
-    sent = far_gradient(mixed, hold(far_weight))
+    arrivals = [paired(own, bits) for bits in (6, 4, 2)]
+    far_weight = hold(far_weight)
+    mixed, far_weight = lax.optimization_barrier((mixed, far_weight))
+    sent = far_gradient(mixed)
     arrived = lax.ppermute(sent, "fsdp", ACROSS)
 
     def second(mixed, own, arrivals, weight, far_weight):

time: 127 us -> 139 us (1.094)
  blocking collectives: 20.5 us -> 37.6 us
  waiting for transfers between devices: 16.9 us -> 13.8 us
  local copies, waits for them, and re-layouts: 1.68 us -> 0.04 us
    all_to_all x1, blocking collectives: 20.5 us -> 37.6 us  [exchange(): lax.all_to_all(rows, axis, split_axis=0, concat_axis=0, tiled=True, axis_...]
    ppermute x1, waiting for transfers between devices: 0.01 us -> 11.3 us  [body(): far_weight = lax.ppermute(weight, 'fsdp', ACROSS)]
    all_to_all x1, waiting for transfers between devices: 10.8 us -> 0.01 us  [exchange(): lax.all_to_all(rows, axis, split_axis=0, concat_axis=0, tiled=True, axis_...]
    ppermute x1, waiting for transfers between devices: 3.62 us -> 0.01 us  [body(): arrived = lax.ppermute(sent, 'fsdp', ACROSS)]
    unnamed x14 -> x10, local copies, waits for them, and re-layouts: 1.66 us -> 0.03 us
  transfers between devices with their start and end apart: 13 -> 13, of which waited for: 3 -> 2; matrix products, arithmetic and copies ran while one was open for 2% -> 1% of each run, Pallas kernels for 8% -> 8%
where the time goes in v5:
time: 139 us; the launch traced here: 138 us
  starting transfers between devices  70.8 us (51%)
  blocking collectives  37.6 us (27%)
  waiting for transfers between devices  13.8 us (10%)
  Pallas kernels  12.1 us (9%)
  other arithmetic  2.03 us (1%)
  between operations  1.5 us (1%)
    all_to_all x1, blocking collectives, exchange(): lax.all_to_all(rows, axis, split_axis=0, concat_axis=0, tiled=True, axis_...  37.6 us
    ppermute x6, starting transfers between devices, turned(): return lax.ppermute(rows, 'replica', ring)  22.8 us
    ppermute x1, starting transfers between devices, body(): arrived = lax.ppermute(sent, 'fsdp', ACROSS)  14.9 us
    ppermute x4, starting transfers between devices, paired(): lax.ppermute(rows, 'replica', [(r, r ^ bits) for r in range(REPLICAS)])  14.6 us
    ppermute x1, starting transfers between devices, body(): far_weight = lax.ppermute(weight, 'fsdp', ACROSS)  13.9 us
    ppermute x1, waiting for transfers between devices, body(): far_weight = lax.ppermute(weight, 'fsdp', ACROSS)  11.3 us
    all_to_all x1, starting transfers between devices, exchange(): lax.all_to_all(rows, axis, split_axis=0, concat_axis=0, tiled=True, axis_...  4.6 us
    pallas_call x1, Pallas kernels, normalise(): pl.pallas_call(norm_kernel, grid_spec=pltpu.PrefetchScalarGridSpec(num_sc...  3.68 us
  transfers between devices with their start and end apart: 13, of which 2 were waited for; matrix products, arithmetic and copies ran while one was open for 1% of the time, Pallas kernels for 8%

profile of v5, /device:TPU:64, one launch (start us, length us, event | category | flops | bytes accessed | tf_op | source)
XLA Modules:
  0.0 138.1 jit_solution(14249541607832716325)
XLA Ops:
  0.6 13.9 %collective-permute-start.6 = (bf16[512,512]{1,0:T(8,128)(2,1)}, bf16[512,512]{1,0:T(8,128)(2,1)S(1)}, u32[]{:S(2)}, u32[]{:S(2)}) collective-permute-start(bf16[512,512]{1,0:T(8,128)(2,1)} %bitcast.10), channel_id=1, source_target_pairs={{0,8},{1,9},{2,10},{3,11},{4,12},{5,13},{6,14},{7,15},{8,0},{9,1},... | collective-permute-start | bytes 1572872 | tf_op jit(solution)/shard_map/ppermute | solution.py:250
  14.6 3.7 %normalise.1 = bf16[8,128,1536]{2,1,0:T(8,128)(2,1)} custom-call(s32[1]{0:T(128)} %bitcast.3.half_ref, bf16[128,8192]{1,0:T(8,128)(2,1)} %acts_ref.1, bf16[64,128]{1,0:T(8,128)(2,1)} %bitcast.13, bf16[128,512]{1,0:T(8,128)(2,1)} %cot_ref.1), custom_call_target="tpu_custom_call" | custom-call | flops 1000000 | bytes 10000 | tf_op jit(solution)/shard_map/normalise/pallas_call | solution.py:63
  18.3 4.6 %all-to-all-start.1 = ((bf16[8,128,1536]{2,1,0:T(8,128)(2,1)}), bf16[8,128,1536]{2,1,0:T(8,128)(2,1)}, u32[]{:S(2)}, u32[]{:S(2)}) async-start(bf16[8,128,1536]{2,1,0:T(8,128)(2,1)} %normalise.1), calls=%async_computation.1 | async-start | bytes 6291456 | tf_op jit(solution)/shard_map/all_to_all | solution.py:170
  23.5 14.0 %conditional.3 = (bf16[128,128]{1,0:T(8,128)(2,1)S(1)}) conditional(s32[]{:T(128)} %bitcast.1, () %tuple.36, bf16[512,128]{1,0:T(8,128)(2,1)S(1)} %bitcast.12), branch_computations={%region_0.1_spmd, %region_1.2_spmd} | conditional | flops 131133 | bytes 754462 | solution.py:166
  23.6 3.4 %collective-permute-start = (bf16[128,128]{1,0:T(8,128)(2,1)S(1)}, bf16[128,128]{1,0:T(8,128)(2,1)S(1)}, u32[]{:S(2)}, u32[]{:S(2)}) collective-permute-start(bf16[128,128]{1,0:T(8,128)(2,1)S(1)} %get-tuple-element.71), channel_id=1, source_target_pairs={{0,128},{16,144},{32,160},{48,176},{64,192},{80,208},{96,224},{112... | collective-permute-start | bytes 98312 | tf_op jit(solution)/shard_map/cond/branch_1_fun/ppermute | solution.py:180
  27.0 4.6 %collective-permute-start.1 = (bf16[128,128]{1,0:T(8,128)(2,1)S(1)}, bf16[128,128]{1,0:T(8,128)(2,1)S(1)}, u32[]{:S(2)}, u32[]{:S(2)}) collective-permute-start(bf16[128,128]{1,0:T(8,128)(2,1)S(1)} %get-tuple-element.73), channel_id=1, source_target_pairs={{0,256},{16,272},{32,288},{48,304},{64,320},{80,336},{96,352},{112... | collective-permute-start | bytes 98312 | tf_op jit(solution)/shard_map/cond/branch_1_fun/ppermute | solution.py:180
  31.7 3.3 %collective-permute-start.2 = (bf16[128,128]{1,0:T(8,128)(2,1)S(1)}, bf16[128,128]{1,0:T(8,128)(2,1)S(1)}, u32[]{:S(2)}, u32[]{:S(2)}) collective-permute-start(bf16[128,128]{1,0:T(8,128)(2,1)S(1)} %get-tuple-element.72), channel_id=1, source_target_pairs={{0,384},{16,400},{32,416},{48,432},{64,448},{80,464},{96,480},{112... | collective-permute-start | bytes 98312 | tf_op jit(solution)/shard_map/cond/branch_1_fun/ppermute | solution.py:180
  35.0 0.0 collective-permute-done
  35.1 2.4 %collective-permute-done.2 = bf16[128,128]{1,0:T(8,128)(2,1)S(1)} collective-permute-done((bf16[128,128]{1,0:T(8,128)(2,1)S(1)}, bf16[128,128]{1,0:T(8,128)(2,1)S(1)}, u32[]{:S(2)}, u32[]{:S(2)}) %collective-permute-start.2) | collective-permute-done | bytes 32800 | tf_op jit(solution)/shard_map/cond/branch_1_fun/ppermute | solution.py:180
  37.5 3.4 %collective-permute-start.7 = (bf16[128,128]{1,0:T(8,128)(2,1)S(1)}, bf16[128,128]{1,0:T(8,128)(2,1)S(1)}, u32[]{:S(2)}, u32[]{:S(2)}) collective-permute-start(bf16[128,128]{1,0:T(8,128)(2,1)S(1)} %get-tuple-element.86), channel_id=1, source_target_pairs={{0,96},{16,112},{32,64},{48,80},{64,32},{80,48},{96,0},{112,16},{1... | collective-permute-start | bytes 98312 | tf_op jit(solution)/shard_map/ppermute | solution.py:184
  40.9 7.3 %collective-permute-start.8 = (bf16[128,128]{1,0:T(8,128)(2,1)S(1)}, bf16[128,128]{1,0:T(8,128)(2,1)S(1)}, u32[]{:S(2)}, u32[]{:S(2)}) collective-permute-start(bf16[128,128]{1,0:T(8,128)(2,1)S(1)} %get-tuple-element.86), channel_id=1, source_target_pairs={{0,64},{16,80},{32,96},{48,112},{64,0},{80,16},{96,32},{112,48},{1... | collective-permute-start | bytes 98312 | tf_op jit(solution)/shard_map/ppermute | solution.py:184
  48.2 1.9 %collective-permute-start.9 = (bf16[128,128]{1,0:T(8,128)(2,1)S(1)}, bf16[128,128]{1,0:T(8,128)(2,1)S(1)}, u32[]{:S(2)}, u32[]{:S(2)}) collective-permute-start(bf16[128,128]{1,0:T(8,128)(2,1)S(1)} %get-tuple-element.86), channel_id=1, source_target_pairs={{0,32},{16,48},{32,0},{48,16},{64,96},{80,112},{96,64},{112,80},{1... | collective-permute-start | bytes 98312 | tf_op jit(solution)/shard_map/ppermute | solution.py:184
  50.1 11.3 %collective-permute-done.6.in_ref = bf16[512,512]{1,0:T(8,128)(2,1)S(1)} collective-permute-done((bf16[512,512]{1,0:T(8,128)(2,1)}, bf16[512,512]{1,0:T(8,128)(2,1)S(1)}, u32[]{:S(2)}, u32[]{:S(2)}) %collective-permute-start.6) | collective-permute-done | bytes 524320 | tf_op jit(solution)/shard_map/ppermute | solution.py:250
  61.5 0.0 all-to-all-done.1
  61.5 0.0 copy-start.2
  61.5 2.4 %far_gradient.1 = bf16[512,512]{1,0:T(8,128)(2,1)S(1)} custom-call(bf16[1024,1536]{1,0:T(8,128)(2,1)} %bitcast.5.normed_ref.cot_ref, bf16[1024,1536]{1,0:T(8,128)(2,1)} %bitcast.5.normed_ref.cot_ref), custom_call_target="tpu_custom_call" | custom-call | flops 1000000 | bytes 10000 | tf_op jit(solution)/shard_map/far_gradient/pallas_call | solution.py:93
  63.9 14.9 %collective-permute-start.10 = (bf16[512,512]{1,0:T(8,128)(2,1)S(1)}, bf16[512,512]{1,0:T(8,128)(2,1)S(1)}, u32[]{:S(2)}, u32[]{:S(2)}) collective-permute-start(bf16[512,512]{1,0:T(8,128)(2,1)S(1)} %far_gradient.1), channel_id=1, source_target_pairs={{0,8},{1,9},{2,10},{3,11},{4,12},{5,13},{6,14},{7,15},{8,0},{9,1},... | collective-permute-start | bytes 1572872 | tf_op jit(solution)/shard_map/ppermute | solution.py:261
  78.9 15.8 %conditional.4 = (bf16[1024,512]{1,0:T(8,128)(2,1)S(1)}, f32[512,512]{1,0:T(8,128)S(1)}, bf16[128,128]{1,0:T(8,128)(2,1)}, bf16[128,128]{1,0:T(8,128)(2,1)}, bf1...) conditional(s32[]{:T(128)} %bitcast.1, () %tuple.33, (bf16[1024,1536]{1,0:T(8,128)(2,1)}, ...), branch_computations={%region_2.3_spmd, %region_3.4_spmd} | conditional | flops 131072 | bytes 2228286 | solution.py:166
  78.9 0.6 add_convert_fusion.1
  79.6 3.4 %collective-permute-start.3 = (bf16[128,128]{1,0:T(8,128)(2,1)}, bf16[128,128]{1,0:T(8,128)(2,1)}, u32[]{:S(2)}, u32[]{:S(2)}) collective-permute-start(bf16[128,128]{1,0:T(8,128)(2,1)} %add_convert_fusion.1), channel_id=1, source_target_pairs={{0,128},{16,144},{32,160},{48,176},{64,192},{80,208},{96,224},{112... | collective-permute-start | bytes 98312 | tf_op jit(solution)/shard_map/cond/branch_1_fun/ppermute | solution.py:180
  83.0 4.6 %collective-permute-start.4 = (bf16[128,128]{1,0:T(8,128)(2,1)}, bf16[128,128]{1,0:T(8,128)(2,1)}, u32[]{:S(2)}, u32[]{:S(2)}) collective-permute-start(bf16[128,128]{1,0:T(8,128)(2,1)} %add_convert_fusion.1), channel_id=1, source_target_pairs={{0,256},{16,272},{32,288},{48,304},{64,320},{80,336},{96,352},{112... | collective-permute-start | bytes 98312 | tf_op jit(solution)/shard_map/cond/branch_1_fun/ppermute | solution.py:180
  87.6 3.3 %collective-permute-start.5 = (bf16[128,128]{1,0:T(8,128)(2,1)}, bf16[128,128]{1,0:T(8,128)(2,1)}, u32[]{:S(2)}, u32[]{:S(2)}) collective-permute-start(bf16[128,128]{1,0:T(8,128)(2,1)} %add_convert_fusion.1), channel_id=1, source_target_pairs={{0,384},{16,400},{32,416},{48,432},{64,448},{80,464},{96,480},{112... | collective-permute-start | bytes 98312 | tf_op jit(solution)/shard_map/cond/branch_1_fun/ppermute | solution.py:180
  91.0 3.7 %near_work.1 = (bf16[1024,512]{1,0:T(8,128)(2,1)S(1)}, f32[512,512]{1,0:T(8,128)S(1)}) custom-call(bf16[1024,1536]{1,0:T(8,128)(2,1)} %get-tuple-element.22.mixed_ref, bf16[512,512]{1,0:T(8,128)(2,1)S(1)} %get-tuple-element.23.near_weight_ref, bf16[512,512]{1,0:T(8,128)(2,1)S(1)} %get-tuple-element.24.far_weight_ref), custom_call_target="tpu_custom_call" | custom-call | tf_op jit(solution)/shard_map/cond/branch_1_fun/near_work/pallas_call | solution.py:119
  94.7 0.8 join.1.ours_ref
  95.5 0.0 copy-start
  95.5 0.0 copy-start.1
  95.5 2.1 %collective-permute-start.11 = (bf16[512,128]{1,0:T(8,128)(2,1)S(1)}, bf16[512,128]{1,0:T(8,128)(2,1)S(1)}, u32[]{:S(2)}, u32[]{:S(2)}) collective-permute-start(bf16[512,128]{1,0:T(8,128)(2,1)S(1)} %join.1.ours_ref), channel_id=1, source_target_pairs={{0,16},{16,0},{32,48},{48,32},{64,80},{80,64},{96,112},{112,96},{1... | collective-permute-start | bytes 393224 | tf_op jit(solution)/shard_map/ppermute | solution.py:184
  97.6 39.0 %conditional.5 = (bf16[128,512]{1,0:T(8,128)(2,1)S(1)}) conditional(s32[]{:T(128)} %bitcast.1, () %tuple.32, bf16[1024,512]{1,0:T(8,128)(2,1)S(1)} %get-tuple-element.62), branch_computations={%region_4.5_spmd, %region_5.7_spmd} | conditional | flops 458752 | bytes 3276810 | solution.py:166
  97.6 37.6 %all_to_all.16 = bf16[8,128,512]{2,1,0:T(8,128)(2,1)} all-to-all(bf16[8,128,512]{2,1,0:T(8,128)(2,1)S(1)} %bitcast.9), channel_id=1, replica_groups={{0,1,2,3,4,5,6,7},{8,9,10,11,12,13,14,15},{16,17,18,19,20,21,22,23},{24..., dimensions={0} | all-to-all | bytes 2097152 | tf_op jit(solution)/shard_map/cond/branch_1_fun/all_to_all | solution.py:170
  135.2 1.4 reduce_sum.11
  136.6 0.0 copy-start.4
  136.7 1.4 %blend.1 = (bf16[512,512]{1,0:T(8,128)(2,1)}, f32[512,128]{1,0:T(8,128)}, f32[512,128]{1,0:T(8,128)}) custom-call(s32[1]{0:T(128)S(6)} %copy.28.start_ref, f32[512,512]{1,0:T(8,128)S(1)} %get-tuple-element.65.stepped_ref, bf16[512,512]{1,0:T(8,128)(2,1)S(1)} %collective-permute-done.10.arrived_ref, bf16[512,128]{1,0:T(8,128)(2,1)S(1)} %join.1.ours_ref, ...), custom_call_target="tpu_custom_call" | custom-call | tf_op jit(solution)/shard_map/blend/pallas_call | solution.py:149
  (18 shorter events, 0.1 us)
Async XLA Ops:
  0.6 60.8 %collective-permute-start.6 = (bf16[512,512]{1,0:T(8,128)(2,1)}, bf16[512,512]{1,0:T(8,128)(2,1)S(1)}, u32[]{:S(2)}, u32[]{:S(2)}) collective-permute-start(bf16[512,512]{1,0:T(8,128)(2,1)} %bitcast.10), channel_id=1, source_target_pairs={{0,8},{1,9},{2,10},{3,11},{4,12},{5,13},{6,14},{7,15},{8,0},{9,1},... | collective-permute-start | bytes 1572872 | tf_op jit(solution)/shard_map/ppermute | solution.py:250
  18.3 5.3 %copy-start.3 = (bf16[1,512,128]{2,1,0:T(8,128)(2,1)S(1)}, bf16[1,512,128]{2,1,0:T(8,128)(2,1)}, u32[]{:S(2)}) copy-start(bf16[1,512,128]{2,1,0:T(8,128)(2,1)} %param.18) | copy-start | bytes 393220
  18.3 43.2 %all-to-all-start.1 = ((bf16[8,128,1536]{2,1,0:T(8,128)(2,1)}), bf16[8,128,1536]{2,1,0:T(8,128)(2,1)}, u32[]{:S(2)}, u32[]{:S(2)}) async-start(bf16[8,128,1536]{2,1,0:T(8,128)(2,1)} %normalise.1), calls=%async_computation.1 | async-start | bytes 6291456 | tf_op jit(solution)/shard_map/all_to_all | solution.py:170
  23.6 11.4 %collective-permute-start = (bf16[128,128]{1,0:T(8,128)(2,1)S(1)}, bf16[128,128]{1,0:T(8,128)(2,1)S(1)}, u32[]{:S(2)}, u32[]{:S(2)}) collective-permute-start(bf16[128,128]{1,0:T(8,128)(2,1)S(1)} %get-tuple-element.71), channel_id=1, source_target_pairs={{0,128},{16,144},{32,160},{48,176},{64,192},{80,208},{96,224},{112... | collective-permute-start | bytes 98312 | tf_op jit(solution)/shard_map/cond/branch_1_fun/ppermute | solution.py:180
  27.0 8.0 %collective-permute-start.1 = (bf16[128,128]{1,0:T(8,128)(2,1)S(1)}, bf16[128,128]{1,0:T(8,128)(2,1)S(1)}, u32[]{:S(2)}, u32[]{:S(2)}) collective-permute-start(bf16[128,128]{1,0:T(8,128)(2,1)S(1)} %get-tuple-element.73), channel_id=1, source_target_pairs={{0,256},{16,272},{32,288},{48,304},{64,320},{80,336},{96,352},{112... | collective-permute-start | bytes 98312 | tf_op jit(solution)/shard_map/cond/branch_1_fun/ppermute | solution.py:180
  31.7 5.8 %collective-permute-start.2 = (bf16[128,128]{1,0:T(8,128)(2,1)S(1)}, bf16[128,128]{1,0:T(8,128)(2,1)S(1)}, u32[]{:S(2)}, u32[]{:S(2)}) collective-permute-start(bf16[128,128]{1,0:T(8,128)(2,1)S(1)} %get-tuple-element.72), channel_id=1, source_target_pairs={{0,384},{16,400},{32,416},{48,432},{64,448},{80,464},{96,480},{112... | collective-permute-start | bytes 98312 | tf_op jit(solution)/shard_map/cond/branch_1_fun/ppermute | solution.py:180
  37.5 41.4 %collective-permute-start.7 = (bf16[128,128]{1,0:T(8,128)(2,1)S(1)}, bf16[128,128]{1,0:T(8,128)(2,1)S(1)}, u32[]{:S(2)}, u32[]{:S(2)}) collective-permute-start(bf16[128,128]{1,0:T(8,128)(2,1)S(1)} %get-tuple-element.86), channel_id=1, source_target_pairs={{0,96},{16,112},{32,64},{48,80},{64,32},{80,48},{96,0},{112,16},{1... | collective-permute-start | bytes 98312 | tf_op jit(solution)/shard_map/ppermute | solution.py:184
  40.9 38.0 %collective-permute-start.8 = (bf16[128,128]{1,0:T(8,128)(2,1)S(1)}, bf16[128,128]{1,0:T(8,128)(2,1)S(1)}, u32[]{:S(2)}, u32[]{:S(2)}) collective-permute-start(bf16[128,128]{1,0:T(8,128)(2,1)S(1)} %get-tuple-element.86), channel_id=1, source_target_pairs={{0,64},{16,80},{32,96},{48,112},{64,0},{80,16},{96,32},{112,48},{1... | collective-permute-start | bytes 98312 | tf_op jit(solution)/shard_map/ppermute | solution.py:184
  48.2 30.7 %collective-permute-start.9 = (bf16[128,128]{1,0:T(8,128)(2,1)S(1)}, bf16[128,128]{1,0:T(8,128)(2,1)S(1)}, u32[]{:S(2)}, u32[]{:S(2)}) collective-permute-start(bf16[128,128]{1,0:T(8,128)(2,1)S(1)} %get-tuple-element.86), channel_id=1, source_target_pairs={{0,32},{16,48},{32,0},{48,16},{64,96},{80,112},{96,64},{112,80},{1... | collective-permute-start | bytes 98312 | tf_op jit(solution)/shard_map/ppermute | solution.py:184
  61.5 17.4 %copy-start.2 = (bf16[1,512,512]{2,1,0:T(8,128)(2,1)S(1)}, bf16[1,512,512]{2,1,0:T(8,128)(2,1)}, u32[]{:S(2)}) copy-start(bf16[1,512,512]{2,1,0:T(8,128)(2,1)} %param.16) | copy-start | bytes 1572868
  63.9 72.7 %collective-permute-start.10 = (bf16[512,512]{1,0:T(8,128)(2,1)S(1)}, bf16[512,512]{1,0:T(8,128)(2,1)S(1)}, u32[]{:S(2)}, u32[]{:S(2)}) collective-permute-start(bf16[512,512]{1,0:T(8,128)(2,1)S(1)} %far_gradient.1), channel_id=1, source_target_pairs={{0,8},{1,9},{2,10},{3,11},{4,12},{5,13},{6,14},{7,15},{8,0},{9,1},... | collective-permute-start | bytes 1572872 | tf_op jit(solution)/shard_map/ppermute | solution.py:261
  79.6 15.1 %collective-permute-start.3 = (bf16[128,128]{1,0:T(8,128)(2,1)}, bf16[128,128]{1,0:T(8,128)(2,1)}, u32[]{:S(2)}, u32[]{:S(2)}) collective-permute-start(bf16[128,128]{1,0:T(8,128)(2,1)} %add_convert_fusion.1), channel_id=1, source_target_pairs={{0,128},{16,144},{32,160},{48,176},{64,192},{80,208},{96,224},{112... | collective-permute-start | bytes 98312 | tf_op jit(solution)/shard_map/cond/branch_1_fun/ppermute | solution.py:180
  83.0 11.7 %collective-permute-start.4 = (bf16[128,128]{1,0:T(8,128)(2,1)}, bf16[128,128]{1,0:T(8,128)(2,1)}, u32[]{:S(2)}, u32[]{:S(2)}) collective-permute-start(bf16[128,128]{1,0:T(8,128)(2,1)} %add_convert_fusion.1), channel_id=1, source_target_pairs={{0,256},{16,272},{32,288},{48,304},{64,320},{80,336},{96,352},{112... | collective-permute-start | bytes 98312 | tf_op jit(solution)/shard_map/cond/branch_1_fun/ppermute | solution.py:180
  87.6 7.1 %collective-permute-start.5 = (bf16[128,128]{1,0:T(8,128)(2,1)}, bf16[128,128]{1,0:T(8,128)(2,1)}, u32[]{:S(2)}, u32[]{:S(2)}) collective-permute-start(bf16[128,128]{1,0:T(8,128)(2,1)} %add_convert_fusion.1), channel_id=1, source_target_pairs={{0,384},{16,400},{32,416},{48,432},{64,448},{80,464},{96,480},{112... | collective-permute-start | bytes 98312 | tf_op jit(solution)/shard_map/cond/branch_1_fun/ppermute | solution.py:180
  95.5 41.1 %copy-start = (f32[512,128]{1,0:T(8,128)S(1)}, f32[512,128]{1,0:T(8,128)}, u32[]{:S(2)}) copy-start(f32[512,128]{1,0:T(8,128)} %frag_ref.1) | copy-start | bytes 786436
  95.5 41.1 %copy-start.1 = (f32[512,128]{1,0:T(8,128)S(1)}, f32[512,128]{1,0:T(8,128)}, u32[]{:S(2)}) copy-start(f32[512,128]{1,0:T(8,128)} %mom_ref.1) | copy-start | bytes 786436
  95.5 41.1 %collective-permute-start.11 = (bf16[512,128]{1,0:T(8,128)(2,1)S(1)}, bf16[512,128]{1,0:T(8,128)(2,1)S(1)}, u32[]{:S(2)}, u32[]{:S(2)}) collective-permute-start(bf16[512,128]{1,0:T(8,128)(2,1)S(1)} %join.1.ours_ref), channel_id=1, source_target_pairs={{0,16},{16,0},{32,48},{48,32},{64,80},{80,64},{96,112},{112,96},{1... | collective-permute-start | bytes 393224 | tf_op jit(solution)/shard_map/ppermute | solution.py:184
  136.6 1.5 %copy-start.4 = (bf16[128,512]{1,0:T(8,128)(2,1)}, bf16[128,512]{1,0:T(8,128)(2,1)S(1)}, u32[]{:S(2)}) copy-start(bf16[128,512]{1,0:T(8,128)(2,1)S(1)} %get-tuple-element.87) | copy-start | bytes 393220
